TPU v7x, 512 devices: a whole 4x8x8 slice. The times are simulated.
512 devices in a mesh: depth: 4 (over y_lo, core), row: 16 (over x, y_hi), col: 8 (over z).
Axes of the slice: x: 4, y: 8 (y_hi: 4, y_lo: 2; y = y_hi * 2 + y_lo), z: 8, core: 2. Of those that a mesh axis runs over, the one named last changes fastest.
Arguments:
- activations: bfloat16 [512, 12288], P(('depth', 'col'), 'row'), may hold values from -6 to 6
- weight_up: bfloat16 [12288, 24576], P('row', ('depth', 'col')), may hold values from -0.0546875 to 0.0546875
- weight_down: bfloat16 [24576, 12288], P(('depth', 'col'), 'row'), may hold values from -0.0390625 to 0.0390625
- out_grad: bfloat16 [512, 12288], P(('depth', 'col'), 'row'), may hold values from -6 to 6
Outputs:
- layer_out: bfloat16 [512, 12288], P(('depth', 'col'), 'row')
- input_grad: bfloat16 [512, 12288], P(('depth', 'col'), 'row')
- up_grad: bfloat16 [12288, 24576], P('row', ('depth', 'col'))
- down_grad: bfloat16 [24576, 12288], P(('depth', 'col'), 'row')
All inputs are finite; a program needn't handle non-finite values.
Results may differ from a plain program's by a relative error of at most 0.0049.
Values may be sent and summed in bfloat16 or wider, within the bound.
A program may use at most 64 MiB of HBM per device.

v0:
```python
import jax
import jax.numpy as jnp
from jax import lax
from jax.sharding import PartitionSpec as P

tanh_scale = 0.7978845608028654
cubic_coeff = 0.044715


def gelu_parts(preact):
    inner = tanh_scale * (preact + cubic_coeff * preact * preact * preact)
    hyper = jnp.tanh(inner)
    activated = 0.5 * preact * (1.0 + hyper)
    derivative = 0.5 * (1.0 + hyper) + 0.5 * preact * (1.0 - hyper * hyper) * tanh_scale * (
        1.0 + 3.0 * cubic_coeff * preact * preact
    )
    return (activated, derivative)


def contract(left, right, left_dim, right_dim):
    return lax.dot_general(
        left, right, (((left_dim,), (right_dim,)), ((), ())), preferred_element_type=jnp.float32
    )


def shards(activations, weight_up, weight_down, out_grad):
    tokens_all, cotan_all = (
        lax.all_gather(activations, ("depth", "col"), axis=0, tiled=True),
        lax.all_gather(out_grad, ("depth", "col"), axis=0, tiled=True),
    )
    partial_pre = jnp.dot(tokens_all, weight_up, preferred_element_type=jnp.float32)
    partial_back = contract(cotan_all, weight_down, 1, 1)
    preact, backed = lax.psum((partial_pre, partial_back), "row")
    activated, derivative = gelu_parts(preact)
    hidden = activated.astype(jnp.bfloat16)
    pre_grad = (backed * derivative).astype(jnp.bfloat16)
    partial_out = jnp.dot(hidden, weight_down, preferred_element_type=jnp.float32)
    partial_input = contract(pre_grad, weight_up, 1, 1)
    up_grad = contract(tokens_all, pre_grad, 0, 0).astype(jnp.bfloat16)
    down_grad = contract(hidden, cotan_all, 0, 0).astype(jnp.bfloat16)
    summed_out, summed_input = (
        lax.psum_scatter(partial_out, ("depth", "col"), scatter_dimension=0, tiled=True),
        lax.psum_scatter(partial_input, ("depth", "col"), scatter_dimension=0, tiled=True),
    )
    return (summed_out.astype(jnp.bfloat16), summed_input.astype(jnp.bfloat16), up_grad, down_grad)


def solution(mesh):
    placed = (
        P(("depth", "col"), "row"),
        P("row", ("depth", "col")),
        P(("depth", "col"), "row"),
        P(("depth", "col"), "row"),
    )
    return jax.shard_map(
        shards,
        mesh=mesh,
        in_specs=placed,
        out_specs=(
            P(("depth", "col"), "row"),
            P(("depth", "col"), "row"),
            P("row", ("depth", "col")),
            P(("depth", "col"), "row"),
        ),
        check_vma=False,
    )
```

profile of v0, /device:TPU:6, one launch (start us, length us, event | category | flops | bytes accessed | tf_op | source)
XLA Modules:
  0.0 587.2 jit_solution(14643591697187471424)
XLA Ops:
  7.2 0.0 copy-start
  7.2 0.0 all-reduce.3.cloned.1.call-start
  7.2 65.5 %all_gather.6 = bf16[512,768]{1,0:T(8,128)(2,1)S(1)} all-gather(bf16[16,768]{1,0:T(8,128)(2,1)} %param.4), channel_id=1, replica_groups=mesh['depth'=4,'row'=16,'col'=8] {'depth','col'}, dimensions={0}, use_global_device_ids=true | all-gather | bytes 811008 | tf_op jit(solution)/shard_map/all_gather | solution.py:28
  72.8 0.0 copy-start.2
  72.8 56.2 %all_gather.7 = bf16[512,768]{1,0:T(8,128)(2,1)S(1)} all-gather(bf16[16,768]{1,0:T(8,128)(2,1)} %param.7), channel_id=1, replica_groups=mesh['depth'=4,'row'=16,'col'=8] {'depth','col'}, dimensions={0}, use_global_device_ids=true | all-gather | bytes 811008 | tf_op jit(solution)/shard_map/all_gather | solution.py:29
  128.9 0.0 copy-done
  128.9 0.0 copy-start.4
  128.9 2.0 fusion.10
  130.9 0.0 copy-done.2
  130.9 0.0 copy-done.4
  130.9 1.9 fusion.9
  132.8 0.0 all-reduce.3.cloned.1.call-update
  132.9 0.0 reduce-scatter.3.cloned.1.call-start
  132.9 199.4 %all-reduce.3.cloned.1.call-done = (f32[512,768]{1,0:T(8,128)}, f32[512,768]{1,0:T(8,128)}) async-done(((f32[512,768]{1,0:T(8,128)}, f32[512,768]{1,0:T(8,128)}), (f32[512,768]{1,0:T(8,128)}, f32[512,768]{1,0:T(8,128)})) %all-reduce.3.cloned.1.call-update) | async-done | bytes 3145744 | tf_op jit(solution)/shard_map/psum | solution.py:33
  332.3 3.6 fusion.8
  335.9 0.0 copy-start.1
  335.9 0.0 reduce-scatter.3.cloned.1.call-update
  335.9 0.0 reduce-scatter.5.cloned.1.call-start
  336.0 1.3 copy-done.1
  337.3 0.0 copy-start.5
  337.3 2.5 fusion.6
  339.8 0.0 copy-start.3
  339.8 0.9 copy-done.3
  340.7 0.0 copy-done.5
  340.7 2.0 fusion.11
  342.7 0.0 reduce-scatter.5.cloned.1.call-update
  342.7 3.2 fusion.7
  345.9 2.4 copy.8
  348.3 2.0 convolution_convert_fusion
  350.2 107.4 %reduce-scatter.3.cloned.1.call-done = f32[16,768]{1,0:T(8,128)} async-done(((f32[512,768]{1,0:T(8,128)}), f32[16,768]{1,0:T(8,128)}) %reduce-scatter.3.cloned.1.call-update) | async-done | bytes 49168 | tf_op jit(solution)/shard_map/reduce_scatter | solution.py:42
  457.6 1.4 convert_element_type.22
  459.0 120.3 %reduce-scatter.5.cloned.1.call-done = f32[16,768]{1,0:T(8,128)} async-done(((f32[512,768]{1,0:T(8,128)}), f32[16,768]{1,0:T(8,128)}) %reduce-scatter.5.cloned.1.call-update) | async-done | bytes 49168 | tf_op jit(solution)/shard_map/reduce_scatter | solution.py:43
  579.3 1.4 convert_element_type.24
Async XLA Ops:
  7.2 121.8 %copy-start = (bf16[768,768]{1,0:T(8,128)(2,1)S(1)}, bf16[768,768]{1,0:T(8,128)(2,1)}, u32[]{:S(2)}) copy-start(bf16[768,768]{1,0:T(8,128)(2,1)} %param.6) | copy-start | bytes 3538948
  7.2 325.1 %all-reduce.3.cloned.1.call-start = ((), (), s32[]{:S(2)}) async-start(), calls=%async_computation.4 | async-start | bytes 6291456 | tf_op jit(solution)/shard_map/psum | solution.py:33
  72.8 58.2 %copy-start.2 = (bf16[512,768]{1,0:T(8,128)(2,1)}, bf16[512,768]{1,0:T(8,128)(2,1)S(1)}, u32[]{:S(2)}) copy-start(bf16[512,768]{1,0:T(8,128)(2,1)S(1)} %all_gather.6) | copy-start | bytes 2359300
  128.9 2.0 copy-start.4
  132.9 324.7 %reduce-scatter.3.cloned.1.call-start = ((), (), s32[]{:S(2)}) async-start(), calls=%async_computation.2 | async-start | bytes 1622016 | tf_op jit(solution)/shard_map/reduce_scatter | solution.py:42
  335.9 1.4 copy-start.1
  335.9 243.3 %reduce-scatter.5.cloned.1.call-start = ((), (), s32[]{:S(2)}) async-start(), calls=%async_computation.3 | async-start | bytes 1622016 | tf_op jit(solution)/shard_map/reduce_scatter | solution.py:43
  337.3 3.4 copy-start.5
  339.8 0.9 copy-start.3
Sparse Core Ops, SparseCore 0:
  133.0 199.2 all-reduce.2
  336.1 121.4 reduce-scatter.2
  460.6 118.6 reduce-scatter.4
where the time goes:
time: 588 us; the launch traced here: 587 us
  waiting for transfers between devices  427 us (73%)
  blocking collectives  122 us (21%)
  matrix products  14.7 us (2%)
  between operations  13.8 us (2%)
    psum x1, waiting for transfers between devices, shards(): preact, backed = lax.psum((partial_pre, partial_back), 'row')  199 us
    reduce_scatter x1, waiting for transfers between devices, shards(): lax.psum_scatter(partial_input, ('depth', 'col'), scatter_dimension=0, ti...  120 us
    reduce_scatter x1, waiting for transfers between devices, shards(): lax.psum_scatter(partial_out, ('depth', 'col'), scatter_dimension=0, tile...  107 us
    all_gather x1, blocking collectives, shards(): lax.all_gather(activations, ('depth', 'col'), axis=0, tiled=True)  65.5 us
    all_gather x1, blocking collectives, shards(): lax.all_gather(out_grad, ('depth', 'col'), axis=0, tiled=True)  56.2 us
  transfers between devices with their start and end apart: 3, of which 3 were waited for; matrix products, arithmetic and copies ran while one was open for 2% of the time, Pallas kernels for 0%

commit v1 on v0

v1 whole, which is shorter than its diff:
```python
import jax
import jax.numpy as jnp
from jax import lax
from jax.experimental import pallas as pl
from jax.experimental.pallas import tpu as pltpu
from jax.sharding import PartitionSpec as P

tanh_scale = 0.7978845608028654
cubic_coeff = 0.044715

OFFSETS = (0, 1, -1, 2, -2, 3, -3, 4)
CHUNKS = 4
BLK = 16


def slot_of(offset):
    return OFFSETS.index(4 if offset == -4 else offset)


def gelu_parts(preact):
    inner = tanh_scale * (preact + cubic_coeff * preact * preact * preact)
    hyper = jnp.tanh(inner)
    activated = 0.5 * preact * (1.0 + hyper)
    derivative = 0.5 * (1.0 + hyper) + 0.5 * preact * (1.0 - hyper * hyper) * tanh_scale * (
        1.0 + 3.0 * cubic_coeff * preact * preact
    )
    return (activated, derivative)


def contract(left, right, left_dim, right_dim):
    return lax.dot_general(
        left, right, (((left_dim,), (right_dim,)), ((), ())), preferred_element_type=jnp.float32
    )


def rows_of(value):
    return value.reshape((-1, value.shape[-1]))


def kernel(
    act_hbm, up_hbm, down_hbm, cot_hbm,
    out_hbm, in_grad_hbm, up_grad_hbm, down_grad_hbm,
    tok, w_up, w_down, acc0, s1, r1, acc2, s2, r2, acc3, s3, r3, acc4, s4, r4,
    hp, part, q0, ky, sy, ry, own, ds, rd, up_out, down_out, small_out,
    load_sem, store_sem, send_sem, recv_sem,
):
    bf16, f32 = jnp.bfloat16, jnp.float32
    width = tok.shape[-1]
    half = width // 2
    depth, row, z = lax.axis_index("depth"), lax.axis_index("row"), lax.axis_index("col")
    yl, k = depth // 2, depth % 2
    x, yh = row // 4, row % 4
    f1x, f2x = (x + x // 2) % 2, x // 2
    f1y, f2y = (yh + yh // 2) % 2, yh // 2
    p1x, p2x = {"row": (x + 1 - 2 * (x % 2)) * 4 + yh}, {"row": (3 - x) * 4 + yh}
    p1y, p2y = {"row": x * 4 + yh + 1 - 2 * (yh % 2)}, {"row": x * 4 + 3 - yh}
    sibling, ypartner = {"depth": yl * 2 + 1 - k}, {"depth": (1 - yl) * 2 + k}

    def along(offset):
        return {"col": (z + offset + 8) % 8}

    partners = [sibling, ypartner, p1x, p2x, p1y, p2y] + [along(o) for o in OFFSETS[1:]]

    started = []

    def send(src, dst, device):
        n = len(started)
        copy = pltpu.make_async_remote_copy(
            src_ref=src, dst_ref=dst, send_sem=send_sem.at[n], recv_sem=recv_sem.at[n],
            device_id=device, device_id_type=pl.DeviceIdType.MESH,
        )
        copy.start()
        started.append(copy)
        return copy

    loads = [
        pltpu.make_async_copy(act_hbm, tok.at[0, 0, k, yl], load_sem.at[0]),
        pltpu.make_async_copy(cot_hbm, tok.at[1, 0, k, yl], load_sem.at[1]),
        pltpu.make_async_copy(up_hbm, w_up, load_sem.at[2]),
        pltpu.make_async_copy(down_hbm, w_down, load_sem.at[3]),
    ]
    for load in loads:
        load.start()
    barrier = pltpu.get_barrier_semaphore()
    for device in partners:
        pl.semaphore_signal(barrier, inc=1, device_id=device, device_id_type=pl.DeviceIdType.MESH)
    pl.semaphore_wait(barrier, len(partners))

    flow, across, shared = {}, {}, {}

    def block(slot, a=slice(None)):
        return tok.at[a, slot, k, yl]

    def hop(offset, way, a=slice(None)):
        target = offset - way
        flow[target] = flow.get(target, []) + [
            send(block(slot_of(offset), a), block(slot_of(target), a), along(way))
        ]

    def cross(slot):
        across[slot] = send(block(slot), block(slot), ypartner)

    def arrive(offset):
        for copy in flow[offset]:
            copy.wait_recv()

    def share(slot):
        across[slot].wait_recv()
        mine = tok.at[:, slot, k]
        shared[slot] = send(mine, mine, sibling)

    wave = {}

    def reduce1(c):
        for slot in (2 * c, 2 * c + 1):
            shared[slot].wait_recv()
        for a in range(2):
            i, f = 2 * c + a, (f1x, f2x)[a]
            rows = rows_of(tok[a, 2 * c : 2 * c + 2])
            value = contract(rows, w_up[...], 1, 0) if a == 0 else contract(rows, w_down[...], 1, 1)
            acc0[i] = value.reshape(acc0.shape[1:])
            s1[i] = (acc0[i, 1 - f] if a == 0 else acc0[i, :, 1 - f]).astype(bf16)
            wave[c, a] = send(s1.at[i], r1.at[i], (p1x, p2x)[a])

    def reduce2(c):
        for a in range(2):
            i, f, g = 2 * c + a, (f1x, f2x)[a], (f2x, f1x)[a]
            wave[c, a].wait_recv()

            def total(n):
                kept = acc0[i, f, n] if a == 0 else acc0[i, n, f]
                return kept + r1[i, n].astype(f32)

            value = total(1 - g).astype(bf16)
            s2[i, :, 0] = value[..., :half]
            s2[i, :, 1] = value[..., half:]
            wave[c, a] = send(s2.at[i], r2.at[i], (p2x, p1x)[a])
            value = total(g)
            acc2[i, :, 0] = value[..., :half]
            acc2[i, :, 1] = value[..., half:]

    def reduce3(c):
        for a in range(2):
            i, f = 2 * c + a, (f1y, f2y)[a]
            wave[c, a].wait_recv()

            def total(n):
                if a == 0:
                    return acc2[i, n] + r2[i, n].astype(f32)
                return acc2[i, :, n] + r2[i, :, n].astype(f32)

            s3[i] = total(1 - f).astype(bf16)
            wave[c, a] = send(s3.at[i], r3.at[i], (p1y, p2y)[a])
            acc3[i] = total(f)

    def reduce4(c):
        for a in range(2):
            i, f = 2 * c + a, (f2y, f1y)[a]
            wave[c, a].wait_recv()
            s4[i] = acc3[i, 1 - f] + r3[i, 1 - f].astype(f32)
            wave[c, a] = send(s4.at[i], r4.at[i], (p2y, p1y)[a])
            acc4[i] = acc3[i, f] + r3[i, f].astype(f32)

    def double(c, step):
        for a in range(2):
            if step > 0:
                wave[c, a].wait_recv()
            if step == 0:
                region, device = hp.at[c, a, f1x, f2x, f1y, f2y], (p2y, p1y)[a]
            elif step == 1:
                region = hp.at[c, a, f1x, f2x, f1y] if a == 0 else hp.at[c, a, f1x, f2x, :, f2y]
                device = (p1y, p2y)[a]
            elif step == 2:
                region, device = hp.at[c, a, f1x, f2x], (p2x, p1x)[a]
            else:
                region = hp.at[c, a, f1x] if a == 0 else hp.at[c, a, :, f2x]
                device = (p1x, p2x)[a]
            wave[c, a] = send(region, region, device)

    def activate(c):
        wave[c, 0].wait_recv()
        wave[c, 1].wait_recv()
        activated, derivative = gelu_parts(acc4[2 * c] + r4[2 * c])
        hp[c, 0, f1x, f2x, f1y, f2y] = activated.astype(bf16)
        backed = acc4[2 * c + 1] + r4[2 * c + 1]
        hp[c, 1, f1x, f2x, f1y, f2y] = (backed * derivative).astype(bf16)
        double(c, 0)

    pair, cut, scattered = {}, {}, []

    def project(c):
        for a in range(2):
            wave[c, a].wait_recv()
            low, high = rows_of(hp[c, a, :, :, :, 0]), rows_of(hp[c, a, :, :, :, 1])
            rows = jnp.concatenate([low, high], axis=1)
            value = contract(rows, w_down[...], 1, 0) if a == 0 else contract(rows, w_up[...], 1, 1)
            part[c, a] = value.reshape(part.shape[2:])
            pair[c, a] = send(part.at[c, a, :, 1 - k], q0.at[c, a], sibling)

    def merge(c):
        for a in range(2):
            pair[c, a].wait_recv()
            sy[c, a] = (part[c, a, :, k, 1 - yl] + q0[c, a, :, 1 - yl]).astype(bf16)
        cut[c] = send(sy.at[c], ry.at[c], ypartner)
        for a in range(2):
            ky[c, a] = part[c, a, :, k, yl] + q0[c, a, :, yl]

    def scatter(c):
        cut[c].wait_recv()
        for s in (1, 0):
            slot = 2 * c + s
            value = ky[c, :, s] + ry[c, :, s].astype(f32)
            if slot == 0:
                own[...] = value
            else:
                ds[slot] = value.astype(bf16)
                scattered.append(send(ds.at[slot], rd.at[slot], along(OFFSETS[slot])))

    stores = []

    def store(src, dst):
        stores.append(pltpu.make_async_copy(src, dst, store_sem.at[len(stores)]))
        stores[-1].start()

    def up_grad(h):
        cols = slice(h * half, (h + 1) * half)
        left, right = rows_of(tok[0]), rows_of(hp[:, 1, :, :, :, h])
        up_out[:, cols] = contract(left, right, 0, 0).astype(bf16)
        store(up_out.at[:, cols], up_grad_hbm.at[:, cols])

    def down_grad(h):
        rows = slice(h * half, (h + 1) * half)
        left, right = rows_of(hp[:, 0, :, :, :, h]), rows_of(tok[1])
        down_out[rows, :] = contract(left, right, 0, 0).astype(bf16)
        store(down_out.at[rows], down_grad_hbm.at[rows])

    loads[0].wait()
    loads[1].wait()
    hop(0, 1)
    hop(0, -1)
    cross(0)
    hop(0, 2)
    hop(0, -2)
    share(0)
    for offset in (1, -1):
        arrive(offset)
        cross(slot_of(offset))
    for offset in (-2, 2):
        way = -offset // 2
        arrive(offset)
        hop(offset, way)
        hop(offset, 2 * way, 0 if way == 1 else 1)
        cross(slot_of(offset))
    share(1)
    loads[2].wait()
    loads[3].wait()
    reduce1(0)
    share(2)
    share(3)
    for offset in (3, -3, 4):
        arrive_keys = (4, -4) if offset == 4 else (offset,)
        for key in arrive_keys:
            arrive(key)
        cross(slot_of(offset))
    stages = [
        reduce1, reduce2, reduce3, reduce4, activate,
        lambda c: double(c, 1), lambda c: double(c, 2), lambda c: double(c, 3),
        project, merge, scatter,
    ]
    last = CHUNKS - 1
    for t in range(1, len(stages) + last):
        for c in range(CHUNKS):
            n = t - c
            if n == 0 and c >= 2:
                share(2 * c)
                share(2 * c + 1)
            if 0 <= n < len(stages):
                stages[n](c)
                if c == last and stages[n] is project:
                    up_grad(0)
                if c == last and stages[n] is merge:
                    up_grad(1)
                    down_grad(0)
    down_grad(1)
    for copy in scattered:
        copy.wait_recv()
    for a, ref in ((0, out_hbm), (1, in_grad_hbm)):
        total = own[a]
        for slot in range(1, 8):
            total = total + rd[slot, a].astype(f32)
        small_out[a] = total.astype(bf16)
        store(small_out.at[a], ref)
    for copy in started:
        copy.wait_send()
    for copy in stores:
        copy.wait()


COPIES = 128


def place(*refs):
    half = (len(refs) - 1) // 2
    copies = [
        pltpu.make_async_copy(src, dst, refs[-1].at[n])
        for n, (src, dst) in enumerate(zip(refs[:half], refs[half:-1]))
    ]
    for copy in copies:
        copy.start()
    for copy in copies:
        copy.wait()


def shards(activations, weight_up, weight_down, out_grad):
    width, hidden = weight_up.shape
    bf16, f32 = jnp.bfloat16, jnp.float32
    assert activations.shape[0] == BLK and width == hidden

    def vmem(lead, kind):
        return pltpu.VMEM(lead + (BLK, width), kind)

    def halves(lead, kind):
        return pltpu.VMEM(lead + (BLK, hidden // 2), kind)

    pieces = 2 * CHUNKS
    scratch = [
        vmem((2, 8, 2, 2), bf16),
        pltpu.VMEM((width, hidden), bf16), pltpu.VMEM((width, hidden), bf16),
        vmem((pieces, 2, 2, 2), f32), vmem((pieces, 2, 2), bf16), vmem((pieces, 2, 2), bf16),
        halves((pieces, 2, 2), f32), halves((pieces, 2, 2), bf16), halves((pieces, 2, 2), bf16),
        halves((pieces, 2), f32), halves((pieces, 2), bf16), halves((pieces, 2), bf16),
        halves((pieces,), f32), halves((pieces,), f32), halves((pieces,), f32),
        halves((CHUNKS, 2, 2, 2, 2, 2), bf16),
        vmem((CHUNKS, 2, 2, 2, 2), f32), vmem((CHUNKS, 2, 2, 2), f32),
        vmem((CHUNKS, 2, 2), f32), vmem((CHUNKS, 2, 2), bf16), vmem((CHUNKS, 2, 2), bf16),
        vmem((2,), f32), vmem((8, 2), bf16), vmem((8, 2), bf16),
        pltpu.VMEM((width, hidden), bf16), pltpu.VMEM((width, hidden), bf16), vmem((2,), bf16),
        pltpu.SemaphoreType.DMA((4,)), pltpu.SemaphoreType.DMA((6,)),
        pltpu.SemaphoreType.DMA((COPIES,)),
        pltpu.SemaphoreType.DMA((COPIES,)),
    ]
    small = jax.ShapeDtypeStruct(activations.shape, bf16)
    large = jax.ShapeDtypeStruct(weight_up.shape, bf16)
    results = pl.pallas_call(
        kernel,
        out_shape=(small, small, large, large),
        in_specs=[pl.BlockSpec(memory_space=pltpu.HBM)] * 4,
        out_specs=[pl.BlockSpec(memory_space=pltpu.HBM)] * 4,
        scratch_shapes=scratch,
        compiler_params=pltpu.CompilerParams(
            collective_id=0, has_side_effects=True, vmem_limit_bytes=VMEM_MIB * 1024 * 1024
        ),
        cost_estimate=pl.CostEstimate(
            flops=12 * 512 * width * hidden, bytes_accessed=8 * width * hidden, transcendentals=0
        ),
        name="layer",
    )(activations, weight_up, weight_down, out_grad)
    return pl.pallas_call(
        place,
        out_shape=(small, small, large, large),
        in_specs=[pl.BlockSpec(memory_space=pltpu.HBM)] * 4,
        out_specs=[pl.BlockSpec(memory_space=pltpu.HBM)] * 4,
        scratch_shapes=[pltpu.SemaphoreType.DMA((4,))],
        compiler_params=pltpu.CompilerParams(vmem_limit_bytes=VMEM_MIB * 1024 * 1024),
        name="place",
    )(*results)


VMEM_MIB = 60


def solution(mesh):
    placed = (
        P(("depth", "col"), "row"),
        P("row", ("depth", "col")),
        P(("depth", "col"), "row"),
        P(("depth", "col"), "row"),
    )
    return jax.shard_map(
        shards,
        mesh=mesh,
        in_specs=placed,
        out_specs=(
            P(("depth", "col"), "row"),
            P(("depth", "col"), "row"),
            P("row", ("depth", "col")),
            P(("depth", "col"), "row"),
        ),
        check_vma=False,
    )
```

time: 588 us -> 167 us (0.28)
  waiting for transfers between devices: 427 us -> 0 us
  Pallas kernels: 0 us -> 166 us
  blocking collectives: 122 us -> 0 us
  matrix products: 14.7 us -> 0 us
  between operations: 13.8 us -> 0.64 us
    reduce_scatter x2 -> x0, waiting for transfers between devices: 228 us -> none  [the longest x1 120 us: shards(): lax.psum_scatter(partial_input, ('depth', 'col'), scatter_dimension=0, ti...]
    psum x1 -> x0, waiting for transfers between devices: 199 us -> none  [shards(): preact, backed = lax.psum((partial_pre, partial_back), 'row')]
    pallas_call x0 -> x2, Pallas kernels: none -> 166 us  [the longest x1 91.7 us: shards(): pl.pallas_call(kernel, out_shape=(small, small, large, large), in_specs=[...]
    all_gather x2 -> x0, blocking collectives: 122 us -> none  [the longest x1 65.5 us: shards(): lax.all_gather(activations, ('depth', 'col'), axis=0, tiled=True)]
    dot_general x6 -> x0, matrix products: 14.7 us -> none  [the longest x4 9.1 us: contract(): lax.dot_general(left, right, (((left_dim,), (right_dim,)), ((), ())), pre...]
  transfers between devices with their start and end apart: 3 -> 0, of which waited for: 3 -> 0; matrix products, arithmetic and copies ran while one was open for 2% -> 0% of each run, Pallas kernels for 0% -> 0%
where the time goes in v1:
time: 167 us; the launch traced here: 166 us
  Pallas kernels  166 us (99%)
    pallas_call x1, Pallas kernels, shards(): pl.pallas_call(kernel, out_shape=(small, small, large, large), in_specs=[...  91.7 us
    pallas_call x1, Pallas kernels, shards(): pl.pallas_call(place, out_shape=(small, small, large, large), in_specs=[p...  74.1 us

profile of v1, /device:TPU:6, one launch (start us, length us, event | category | flops | bytes accessed | tf_op | source)
XLA Modules:
  0.0 166.4 jit_solution(12470250079585529094)
XLA Ops:
  0.6 91.7 %layer.1 = (bf16[16,768]{1,0:T(8,128)(2,1)}, bf16[16,768]{1,0:T(8,128)(2,1)}, bf16[768,768]{1,0:T(8,128)(2,1)}, bf16[768,768]{1,0:T(8,128)(2,1)}) custom-call(bf16[16,768]{1,0:T(8,128)(2,1)} %act_hbm.1, bf16[768,768]{1,0:T(8,128)(2,1)} %up_hbm.1, bf16[768,768]{1,0:T(8,128)(2,1)} %down_hbm.1, bf16[16,768]{1,0:T(8,128)(2,1)} %cot_hbm.1), custom_call_target="tpu_custom_call" | custom-call | flops 3623878656 | bytes 4718592 | tf_op jit(solution)/shard_map/layer/pallas_call | solution.py:344
  92.3 74.1 %place.1 = (bf16[16,768]{1,0:T(8,128)(2,1)}, bf16[16,768]{1,0:T(8,128)(2,1)}, bf16[768,768]{1,0:T(8,128)(2,1)}, bf16[768,768]{1,0:T(8,128)(2,1)}) custom-call(bf16[16,768]{1,0:T(8,128)(2,1)} %get-tuple-element.8.refs_0_, bf16[16,768]{1,0:T(8,128)(2,1)} %get-tuple-element.9.refs_1_, bf16[768,768]{1,0:T(8,128)(2,1)} %get-tuple-element.10.refs_2_, ...), custom_call_target="tpu_custom_call" | custom-call | tf_op jit(solution)/shard_map/place/pallas_call | solution.py:358

commit v2 on v1

--- a/solution.py
+++ b/solution.py
@@ -11,6 +11,19 @@
 OFFSETS = (0, 1, -1, 2, -2, 3, -3, 4)
 CHUNKS = 4
 BLK = 16
+
+
+ORDER = (
+    ("y", 1), ("s", 0), ("y", -1), ("s", 1), ("y", 2), ("y", -2), ("s", 2),
+    ("r1", 0), ("s", 3), ("y", 3), ("r1", 1), ("y", 4), ("y", -3), ("s", 4),
+    ("s", 5), ("r2", 0), ("r1", 2), ("s", 6), ("s", 7), ("r2", 1), ("r3", 0),
+    ("r1", 3), ("r2", 2), ("r3", 1), ("r4", 0), ("r2", 3), ("r3", 2), ("r4", 1),
+    ("r3", 3), ("r4", 2), ("act", 1), ("r4", 3), ("act", 2), ("c1", 1), ("act", 0),
+    ("c1", 2), ("c2", 1), ("act", 3), ("c2", 2), ("c3", 1), ("c1", 3), ("c3", 2),
+    ("c1", 0), ("c2", 3), ("p", 1), ("c2", 0), ("p", 2), ("c3", 3), ("m", 1),
+    ("c3", 0), ("m", 2), ("p", 3), ("z", 1), ("p", 0), ("z", 2), ("m", 3),
+    ("g", 3), ("g", 1), ("m", 0), ("z", 3), ("g", 0), ("g", 2), ("z", 0),
+)
 
 
 def slot_of(offset):
@@ -234,54 +247,38 @@
         down_out[rows, :] = contract(left, right, 0, 0).astype(bf16)
         store(down_out.at[rows], down_grad_hbm.at[rows])
 
-    loads[0].wait()
-    loads[1].wait()
-    hop(0, 1)
-    hop(0, -1)
-    cross(0)
-    hop(0, 2)
-    hop(0, -2)
-    share(0)
-    for offset in (1, -1):
+    def begin():
+        loads[0].wait()
+        loads[1].wait()
+        hop(0, 1)
+        hop(0, -1)
+        cross(0)
+        hop(0, 2)
+        hop(0, -2)
+
+    def pass_on(offset):
         arrive(offset)
+        if offset == 4:
+            arrive(-4)
+        if offset in (2, -2):
+            way = -offset // 2
+            hop(offset, way)
+            hop(offset, 2 * way, 0 if way == 1 else 1)
         cross(slot_of(offset))
-    for offset in (-2, 2):
-        way = -offset // 2
-        arrive(offset)
-        hop(offset, way)
-        hop(offset, 2 * way, 0 if way == 1 else 1)
-        cross(slot_of(offset))
-    share(1)
+
+    def grads(n):
+        (up_grad, down_grad)[n // 2](n % 2)
+
+    stages = {
+        "y": pass_on, "s": share, "r1": reduce1, "r2": reduce2, "r3": reduce3, "r4": reduce4,
+        "act": activate, "c1": lambda c: double(c, 1), "c2": lambda c: double(c, 2),
+        "c3": lambda c: double(c, 3), "p": project, "m": merge, "z": scatter, "g": grads,
+    }
+    begin()
     loads[2].wait()
     loads[3].wait()
-    reduce1(0)
-    share(2)
-    share(3)
-    for offset in (3, -3, 4):
-        arrive_keys = (4, -4) if offset == 4 else (offset,)
-        for key in arrive_keys:
-            arrive(key)
-        cross(slot_of(offset))
-    stages = [
-        reduce1, reduce2, reduce3, reduce4, activate,
-        lambda c: double(c, 1), lambda c: double(c, 2), lambda c: double(c, 3),
-        project, merge, scatter,
-    ]
-    last = CHUNKS - 1
-    for t in range(1, len(stages) + last):
-        for c in range(CHUNKS):
-            n = t - c
-            if n == 0 and c >= 2:
-                share(2 * c)
-                share(2 * c + 1)
-            if 0 <= n < len(stages):
-                stages[n](c)
-                if c == last and stages[n] is project:
-                    up_grad(0)
-                if c == last and stages[n] is merge:
-                    up_grad(1)
-                    down_grad(0)
-    down_grad(1)
+    for stage, index in ORDER:
+        stages[stage](index)
     for copy in scattered:
         copy.wait_recv()
     for a, ref in ((0, out_hbm), (1, in_grad_hbm)):
@@ -300,15 +297,22 @@
 
 
 def place(*refs):
-    half = (len(refs) - 1) // 2
-    copies = [
-        pltpu.make_async_copy(src, dst, refs[-1].at[n])
-        for n, (src, dst) in enumerate(zip(refs[:half], refs[half:-1]))
-    ]
-    for copy in copies:
-        copy.start()
-    for copy in copies:
-        copy.wait()
+    arrays, results, buffers, load_sem, store_sem = refs[:4], refs[4:8], refs[8:12], refs[12], refs[13]
+    loads, stores = [], []
+    for src, dst, buffer in zip(arrays, results, buffers):
+        rows = src.shape[0]
+        step = min(rows, 256)
+        for first in range(0, rows, step):
+            n, part = len(loads), pl.ds(first, step)
+            loads.append(pltpu.make_async_copy(src.at[part], buffer.at[part], load_sem.at[n]))
+            stores.append(pltpu.make_async_copy(buffer.at[part], dst.at[part], store_sem.at[n]))
+    for load in loads:
+        load.start()
+    for load, store in zip(loads, stores):
+        load.wait()
+        store.start()
+    for store in stores:
+        store.wait()
 
 
 def shards(activations, weight_up, weight_down, out_grad):
@@ -355,15 +359,18 @@
         ),
         name="layer",
     )(activations, weight_up, weight_down, out_grad)
-    return pl.pallas_call(
+    out, in_grad, up_grad, down_grad = results
+    up_grad, down_grad, out, in_grad = pl.pallas_call(
         place,
-        out_shape=(small, small, large, large),
+        out_shape=(large, large, small, small),
         in_specs=[pl.BlockSpec(memory_space=pltpu.HBM)] * 4,
         out_specs=[pl.BlockSpec(memory_space=pltpu.HBM)] * 4,
-        scratch_shapes=[pltpu.SemaphoreType.DMA((4,))],
+        scratch_shapes=[pltpu.VMEM(result.shape, bf16) for result in (large, large, small, small)]
+        + [pltpu.SemaphoreType.DMA((8,)), pltpu.SemaphoreType.DMA((8,))],
         compiler_params=pltpu.CompilerParams(vmem_limit_bytes=VMEM_MIB * 1024 * 1024),
         name="place",
-    )(*results)
+    )(up_grad, down_grad, out, in_grad)
+    return out, in_grad, up_grad, down_grad
 
 
 VMEM_MIB = 60

time: 167 us -> 86.5 us (0.52)
  Pallas kernels: 166 us -> 85.5 us
    pallas_call x1, Pallas kernels: 74.1 us -> 2.53 us  [shards(): pl.pallas_call(place, out_shape=(large, large, small, small), in_specs=[p...]
    pallas_call x1, Pallas kernels: 91.7 us -> 83 us  [shards(): pl.pallas_call(kernel, out_shape=(small, small, large, large), in_specs=[...]
where the time goes in v2:
time: 86.5 us; the launch traced here: 86.2 us
  Pallas kernels  85.5 us (99%)
    pallas_call x1, Pallas kernels, shards(): pl.pallas_call(kernel, out_shape=(small, small, large, large), in_specs=[...  83 us
    pallas_call x1, Pallas kernels, shards(): pl.pallas_call(place, out_shape=(large, large, small, small), in_specs=[p...  2.53 us

profile of v2, /device:TPU:6, one launch (start us, length us, event | category | flops | bytes accessed | tf_op | source)
XLA Modules:
  0.0 86.2 jit_solution(7214440704816480741)
XLA Ops:
  0.6 83.0 %layer.1 = (bf16[16,768]{1,0:T(8,128)(2,1)}, bf16[16,768]{1,0:T(8,128)(2,1)}, bf16[768,768]{1,0:T(8,128)(2,1)}, bf16[768,768]{1,0:T(8,128)(2,1)}) custom-call(bf16[16,768]{1,0:T(8,128)(2,1)} %act_hbm.1, bf16[768,768]{1,0:T(8,128)(2,1)} %up_hbm.1, bf16[768,768]{1,0:T(8,128)(2,1)} %down_hbm.1, bf16[16,768]{1,0:T(8,128)(2,1)} %cot_hbm.1), custom_call_target="tpu_custom_call" | custom-call | flops 3623878656 | bytes 4718592 | tf_op jit(solution)/shard_map/layer/pallas_call | solution.py:348
  83.6 2.5 %place.1 = (bf16[768,768]{1,0:T(8,128)(2,1)}, bf16[768,768]{1,0:T(8,128)(2,1)}, bf16[16,768]{1,0:T(8,128)(2,1)}, bf16[16,768]{1,0:T(8,128)(2,1)}) custom-call(bf16[768,768]{1,0:T(8,128)(2,1)} %get-tuple-element.12.refs_0_, bf16[768,768]{1,0:T(8,128)(2,1)} %get-tuple-element.13.refs_1_, bf16[16,768]{1,0:T(8,128)(2,1)} %get-tuple-element.14.refs_2_, ...), custom_call_target="tpu_custom_call" | custom-call | tf_op jit(solution)/shard_map/place/pallas_call | solution.py:363

commit v3 on v2

--- a/solution.py
+++ b/solution.py
@@ -14,15 +14,24 @@
 
 
 ORDER = (
-    ("y", 1), ("s", 0), ("y", -1), ("s", 1), ("y", 2), ("y", -2), ("s", 2),
-    ("r1", 0), ("s", 3), ("y", 3), ("r1", 1), ("y", 4), ("y", -3), ("s", 4),
-    ("s", 5), ("r2", 0), ("r1", 2), ("s", 6), ("s", 7), ("r2", 1), ("r3", 0),
-    ("r1", 3), ("r2", 2), ("r3", 1), ("r4", 0), ("r2", 3), ("r3", 2), ("r4", 1),
-    ("r3", 3), ("r4", 2), ("act", 1), ("r4", 3), ("act", 2), ("c1", 1), ("act", 0),
-    ("c1", 2), ("c2", 1), ("act", 3), ("c2", 2), ("c3", 1), ("c1", 3), ("c3", 2),
-    ("c1", 0), ("c2", 3), ("p", 1), ("c2", 0), ("p", 2), ("c3", 3), ("m", 1),
-    ("c3", 0), ("m", 2), ("p", 3), ("z", 1), ("p", 0), ("z", 2), ("m", 3),
-    ("g", 3), ("g", 1), ("m", 0), ("z", 3), ("g", 0), ("g", 2), ("z", 0),
+    ("t", 0), ("y", 1), ("s", 0), ("y", -1), ("s", 1), ("y", 2),
+    ("y", -2), ("s", 2), ("r1", 0, 0), ("r1", 0, 1), ("y", 3), ("s", 3),
+    ("y", -3), ("r1", 1, 0), ("s", 4), ("r1", 1, 1), ("s", 5), ("y", 4),
+    ("r1", 2, 0), ("s", 6), ("r1", 2, 1), ("r2", 0, 1), ("s", 7), ("r2", 1, 0),
+    ("r2", 1, 1), ("r2", 2, 0), ("r1", 3, 1), ("r2", 2, 1), ("r3", 0, 1), ("r1", 3, 0),
+    ("r3", 1, 0), ("r3", 1, 1), ("r3", 2, 0), ("r2", 0, 0), ("r3", 2, 1), ("r4", 1, 0),
+    ("r4", 1, 1), ("r4", 2, 0), ("r2", 3, 1), ("r4", 2, 1), ("r2", 3, 0), ("r3", 0, 0),
+    ("act", 1), ("r3", 3, 1), ("r3", 3, 0), ("act", 2), ("ta", 2), ("c1", 1, 0),
+    ("c1", 1, 1), ("r4", 3, 1), ("r4", 3, 0), ("c1", 2, 0), ("r4", 0, 0), ("c2", 1, 0),
+    ("r4", 0, 1), ("c1", 2, 1), ("c2", 1, 1), ("act", 3), ("c3", 1, 0), ("c2", 2, 0),
+    ("t", 1), ("act", 0), ("c3", 1, 1), ("c2", 2, 1), ("c1", 3, 0), ("c1", 3, 1),
+    ("c3", 2, 0), ("p", 1, 0), ("c1", 0, 0), ("c1", 0, 1), ("c2", 3, 0), ("c3", 2, 1),
+    ("c2", 3, 1), ("p", 1, 1), ("m", 1, 0), ("c2", 0, 0), ("c3", 3, 0), ("p", 2, 0),
+    ("m", 1, 1), ("c2", 0, 1), ("c3", 3, 1), ("p", 2, 1), ("m", 2, 0), ("c3", 0, 0),
+    ("z", 1), ("p", 3, 0), ("m", 2, 1), ("p", 3, 1), ("c3", 0, 1), ("m", 3, 0),
+    ("z", 2), ("p", 0, 0), ("m", 3, 1), ("ta", 3), ("ta", 1), ("ta", 0),
+    ("p", 0, 1), ("z", 3), ("m", 0, 0), ("g", 3), ("m", 0, 1), ("g", 1),
+    ("g", 0), ("z", 0), ("g", 2),
 )
 
 
@@ -53,7 +62,7 @@
 def kernel(
     act_hbm, up_hbm, down_hbm, cot_hbm,
     out_hbm, in_grad_hbm, up_grad_hbm, down_grad_hbm,
-    tok, w_up, w_down, acc0, s1, r1, acc2, s2, r2, acc3, s3, r3, acc4, s4, r4,
+    tok, act_t, w_up, w_down, w_up_t, w_down_t, acc0, s1, r1, acc2, s2, r2, acc3, s3, r3, acc4, s4, r4,
     hp, part, q0, ky, sy, ry, own, ds, rd, up_out, down_out, small_out,
     load_sem, store_sem, send_sem, recv_sem,
 ):
@@ -122,104 +131,109 @@
         mine = tok.at[:, slot, k]
         shared[slot] = send(mine, mine, sibling)
 
-    wave = {}
-
-    def reduce1(c):
+    wave, joined = {}, []
+
+    def flip(which):
+        if which == 0:
+            w_down_t[...] = w_down[...].T
+        else:
+            w_up_t[...] = w_up[...].T
+
+    def flip_tokens(c):
+        act_t[:, c * 8 * BLK : (c + 1) * 8 * BLK] = rows_of(tok[0, 2 * c : 2 * c + 2]).T
+
+    def reduce1(c, a):
         for slot in (2 * c, 2 * c + 1):
-            shared[slot].wait_recv()
-        for a in range(2):
-            i, f = 2 * c + a, (f1x, f2x)[a]
-            rows = rows_of(tok[a, 2 * c : 2 * c + 2])
-            value = contract(rows, w_up[...], 1, 0) if a == 0 else contract(rows, w_down[...], 1, 1)
-            acc0[i] = value.reshape(acc0.shape[1:])
-            s1[i] = (acc0[i, 1 - f] if a == 0 else acc0[i, :, 1 - f]).astype(bf16)
-            wave[c, a] = send(s1.at[i], r1.at[i], (p1x, p2x)[a])
-
-    def reduce2(c):
-        for a in range(2):
-            i, f, g = 2 * c + a, (f1x, f2x)[a], (f2x, f1x)[a]
+            if slot not in joined:
+                shared[slot].wait_recv()
+                joined.append(slot)
+        i, f = 2 * c + a, (f1x, f2x)[a]
+        rows = rows_of(tok[a, 2 * c : 2 * c + 2])
+        value = contract(rows, (w_up, w_down_t)[a][...], 1, 0)
+        acc0[i] = value.reshape(acc0.shape[1:])
+        s1[i] = (acc0[i, 1 - f] if a == 0 else acc0[i, :, 1 - f]).astype(bf16)
+        wave[c, a] = send(s1.at[i], r1.at[i], (p1x, p2x)[a])
+
+    def reduce2(c, a):
+        i, f, g = 2 * c + a, (f1x, f2x)[a], (f2x, f1x)[a]
+        wave[c, a].wait_recv()
+
+        def total(n):
+            kept = acc0[i, f, n] if a == 0 else acc0[i, n, f]
+            return kept + r1[i, n].astype(f32)
+
+        value = total(1 - g).astype(bf16)
+        s2[i, :, 0] = value[..., :half]
+        s2[i, :, 1] = value[..., half:]
+        wave[c, a] = send(s2.at[i], r2.at[i], (p2x, p1x)[a])
+        value = total(g)
+        acc2[i, :, 0] = value[..., :half]
+        acc2[i, :, 1] = value[..., half:]
+
+    def reduce3(c, a):
+        i, f = 2 * c + a, (f1y, f2y)[a]
+        wave[c, a].wait_recv()
+
+        def total(n):
+            if a == 0:
+                return acc2[i, n] + r2[i, n].astype(f32)
+            return acc2[i, :, n] + r2[i, :, n].astype(f32)
+
+        s3[i] = total(1 - f).astype(bf16)
+        wave[c, a] = send(s3.at[i], r3.at[i], (p1y, p2y)[a])
+        acc3[i] = total(f)
+
+    def reduce4(c, a):
+        i, f = 2 * c + a, (f2y, f1y)[a]
+        wave[c, a].wait_recv()
+        s4[i] = acc3[i, 1 - f] + r3[i, 1 - f].astype(f32)
+        wave[c, a] = send(s4.at[i], r4.at[i], (p2y, p1y)[a])
+        acc4[i] = acc3[i, f] + r3[i, f].astype(f32)
+
+    def double(c, a, step):
+        if step > 0:
             wave[c, a].wait_recv()
-
-            def total(n):
-                kept = acc0[i, f, n] if a == 0 else acc0[i, n, f]
-                return kept + r1[i, n].astype(f32)
-
-            value = total(1 - g).astype(bf16)
-            s2[i, :, 0] = value[..., :half]
-            s2[i, :, 1] = value[..., half:]
-            wave[c, a] = send(s2.at[i], r2.at[i], (p2x, p1x)[a])
-            value = total(g)
-            acc2[i, :, 0] = value[..., :half]
-            acc2[i, :, 1] = value[..., half:]
-
-    def reduce3(c):
-        for a in range(2):
-            i, f = 2 * c + a, (f1y, f2y)[a]
-            wave[c, a].wait_recv()
-
-            def total(n):
-                if a == 0:
-                    return acc2[i, n] + r2[i, n].astype(f32)
-                return acc2[i, :, n] + r2[i, :, n].astype(f32)
-
-            s3[i] = total(1 - f).astype(bf16)
-            wave[c, a] = send(s3.at[i], r3.at[i], (p1y, p2y)[a])
-            acc3[i] = total(f)
-
-    def reduce4(c):
-        for a in range(2):
-            i, f = 2 * c + a, (f2y, f1y)[a]
-            wave[c, a].wait_recv()
-            s4[i] = acc3[i, 1 - f] + r3[i, 1 - f].astype(f32)
-            wave[c, a] = send(s4.at[i], r4.at[i], (p2y, p1y)[a])
-            acc4[i] = acc3[i, f] + r3[i, f].astype(f32)
-
-    def double(c, step):
-        for a in range(2):
-            if step > 0:
-                wave[c, a].wait_recv()
-            if step == 0:
-                region, device = hp.at[c, a, f1x, f2x, f1y, f2y], (p2y, p1y)[a]
-            elif step == 1:
-                region = hp.at[c, a, f1x, f2x, f1y] if a == 0 else hp.at[c, a, f1x, f2x, :, f2y]
-                device = (p1y, p2y)[a]
-            elif step == 2:
-                region, device = hp.at[c, a, f1x, f2x], (p2x, p1x)[a]
-            else:
-                region = hp.at[c, a, f1x] if a == 0 else hp.at[c, a, :, f2x]
-                device = (p1x, p2x)[a]
-            wave[c, a] = send(region, region, device)
+        if step == 0:
+            region, device = hp.at[c, a, f1x, f2x, f1y, f2y], (p2y, p1y)[a]
+        elif step == 1:
+            region = hp.at[c, a, f1x, f2x, f1y] if a == 0 else hp.at[c, a, f1x, f2x, :, f2y]
+            device = (p1y, p2y)[a]
+        elif step == 2:
+            region, device = hp.at[c, a, f1x, f2x], (p2x, p1x)[a]
+        else:
+            region = hp.at[c, a, f1x] if a == 0 else hp.at[c, a, :, f2x]
+            device = (p1x, p2x)[a]
+        wave[c, a] = send(region, region, device)
 
     def activate(c):
         wave[c, 0].wait_recv()
         wave[c, 1].wait_recv()
         activated, derivative = gelu_parts(acc4[2 * c] + r4[2 * c])
         hp[c, 0, f1x, f2x, f1y, f2y] = activated.astype(bf16)
+        double(c, 0, 0)
         backed = acc4[2 * c + 1] + r4[2 * c + 1]
         hp[c, 1, f1x, f2x, f1y, f2y] = (backed * derivative).astype(bf16)
-        double(c, 0)
+        double(c, 1, 0)
 
     pair, cut, scattered = {}, {}, []
 
-    def project(c):
-        for a in range(2):
-            wave[c, a].wait_recv()
-            low, high = rows_of(hp[c, a, :, :, :, 0]), rows_of(hp[c, a, :, :, :, 1])
-            rows = jnp.concatenate([low, high], axis=1)
-            value = contract(rows, w_down[...], 1, 0) if a == 0 else contract(rows, w_up[...], 1, 1)
-            part[c, a] = value.reshape(part.shape[2:])
-            pair[c, a] = send(part.at[c, a, :, 1 - k], q0.at[c, a], sibling)
-
-    def merge(c):
-        for a in range(2):
-            pair[c, a].wait_recv()
-            sy[c, a] = (part[c, a, :, k, 1 - yl] + q0[c, a, :, 1 - yl]).astype(bf16)
-        cut[c] = send(sy.at[c], ry.at[c], ypartner)
-        for a in range(2):
-            ky[c, a] = part[c, a, :, k, yl] + q0[c, a, :, yl]
+    def project(c, a):
+        wave[c, a].wait_recv()
+        low, high = rows_of(hp[c, a, :, :, :, 0]), rows_of(hp[c, a, :, :, :, 1])
+        rows = jnp.concatenate([low, high], axis=1)
+        value = contract(rows, (w_down, w_up_t)[a][...], 1, 0)
+        part[c, a] = value.reshape(part.shape[2:])
+        pair[c, a] = send(part.at[c, a, :, 1 - k], q0.at[c, a], sibling)
+
+    def merge(c, a):
+        pair[c, a].wait_recv()
+        sy[c, a] = (part[c, a, :, k, 1 - yl] + q0[c, a, :, 1 - yl]).astype(bf16)
+        cut[c, a] = send(sy.at[c, a], ry.at[c, a], ypartner)
+        ky[c, a] = part[c, a, :, k, yl] + q0[c, a, :, yl]
 
     def scatter(c):
-        cut[c].wait_recv()
+        cut[c, 0].wait_recv()
+        cut[c, 1].wait_recv()
         for s in (1, 0):
             slot = 2 * c + s
             value = ky[c, :, s] + ry[c, :, s].astype(f32)
@@ -237,8 +251,8 @@
 
     def up_grad(h):
         cols = slice(h * half, (h + 1) * half)
-        left, right = rows_of(tok[0]), rows_of(hp[:, 1, :, :, :, h])
-        up_out[:, cols] = contract(left, right, 0, 0).astype(bf16)
+        right = rows_of(hp[:, 1, :, :, :, h])
+        up_out[:, cols] = contract(act_t[...], right, 1, 0).astype(bf16)
         store(up_out.at[:, cols], up_grad_hbm.at[:, cols])
 
     def down_grad(h):
@@ -270,15 +284,16 @@
         (up_grad, down_grad)[n // 2](n % 2)
 
     stages = {
-        "y": pass_on, "s": share, "r1": reduce1, "r2": reduce2, "r3": reduce3, "r4": reduce4,
-        "act": activate, "c1": lambda c: double(c, 1), "c2": lambda c: double(c, 2),
-        "c3": lambda c: double(c, 3), "p": project, "m": merge, "z": scatter, "g": grads,
+        "y": pass_on, "s": share, "t": flip, "ta": flip_tokens, "r1": reduce1, "r2": reduce2,
+        "r3": reduce3, "r4": reduce4, "act": activate, "c1": lambda c, a: double(c, a, 1),
+        "c2": lambda c, a: double(c, a, 2), "c3": lambda c, a: double(c, a, 3),
+        "p": project, "m": merge, "z": scatter, "g": grads,
     }
     begin()
     loads[2].wait()
     loads[3].wait()
-    for stage, index in ORDER:
-        stages[stage](index)
+    for stage, *where in ORDER:
+        stages[stage](*where)
     for copy in scattered:
         copy.wait_recv()
     for a, ref in ((0, out_hbm), (1, in_grad_hbm)):
@@ -329,6 +344,8 @@
     pieces = 2 * CHUNKS
     scratch = [
         vmem((2, 8, 2, 2), bf16),
+        pltpu.VMEM((width, 8 * CHUNKS * BLK), bf16),
+        pltpu.VMEM((width, hidden), bf16), pltpu.VMEM((width, hidden), bf16),
         pltpu.VMEM((width, hidden), bf16), pltpu.VMEM((width, hidden), bf16),
         vmem((pieces, 2, 2, 2), f32), vmem((pieces, 2, 2), bf16), vmem((pieces, 2, 2), bf16),
         halves((pieces, 2, 2), f32), halves((pieces, 2, 2), bf16), halves((pieces, 2, 2), bf16),

time: 86.5 us -> 87.9 us (1.016)
  Pallas kernels: 85.5 us -> 86.4 us
where the time goes in v3:
time: 87.9 us; the launch traced here: 87 us
  Pallas kernels  86.4 us (98%)
    pallas_call x1, Pallas kernels, shards(): pl.pallas_call(kernel, out_shape=(small, small, large, large), in_specs=[...  83.9 us
    pallas_call x1, Pallas kernels, shards(): pl.pallas_call(place, out_shape=(large, large, small, small), in_specs=[p...  2.53 us

profile of v3, /device:TPU:6, one launch (start us, length us, event | category | flops | bytes accessed | tf_op | source)
XLA Modules:
  0.0 87.0 jit_solution(10525494351414433190)
XLA Ops:
  0.6 83.9 %layer.1 = (bf16[16,768]{1,0:T(8,128)(2,1)}, bf16[16,768]{1,0:T(8,128)(2,1)}, bf16[768,768]{1,0:T(8,128)(2,1)}, bf16[768,768]{1,0:T(8,128)(2,1)}) custom-call(bf16[16,768]{1,0:T(8,128)(2,1)} %act_hbm.1, bf16[768,768]{1,0:T(8,128)(2,1)} %up_hbm.1, bf16[768,768]{1,0:T(8,128)(2,1)} %down_hbm.1, bf16[16,768]{1,0:T(8,128)(2,1)} %cot_hbm.1), custom_call_target="tpu_custom_call" | custom-call | flops 3623878656 | bytes 4718592 | tf_op jit(solution)/shard_map/layer/pallas_call | solution.py:365
  84.5 2.5 %place.1 = (bf16[768,768]{1,0:T(8,128)(2,1)}, bf16[768,768]{1,0:T(8,128)(2,1)}, bf16[16,768]{1,0:T(8,128)(2,1)}, bf16[16,768]{1,0:T(8,128)(2,1)}) custom-call(bf16[768,768]{1,0:T(8,128)(2,1)} %get-tuple-element.12.refs_0_, bf16[768,768]{1,0:T(8,128)(2,1)} %get-tuple-element.13.refs_1_, bf16[16,768]{1,0:T(8,128)(2,1)} %get-tuple-element.14.refs_2_, ...), custom_call_target="tpu_custom_call" | custom-call | tf_op jit(solution)/shard_map/place/pallas_call | solution.py:380

commit v4 on v3

v4 whole, which is shorter than its diff:
```python
import jax
import jax.numpy as jnp
from jax import lax
from jax.experimental import pallas as pl
from jax.experimental.pallas import tpu as pltpu
from jax.sharding import PartitionSpec as P

tanh_scale = 0.7978845608028654
cubic_coeff = 0.044715

OFFSETS = (0, 1, -1, 2, -2, 3, -3, 4)
CHUNKS = 4
BLK = 16


ORDER = (
    ("y", 1), ("y", -1), ("y", 2), ("s", 0), ("y", -2), ("y", 3),
    ("s", 1), ("r1", 0, 0), ("r1", 0, 1), ("y", -3), ("y", 4), ("r1", 1, 0),
    ("r1", 1, 1), ("s", 2), ("r2", 0, 0), ("s", 3), ("r2", 0, 1), ("r2", 1, 0),
    ("r2", 1, 1), ("r1", 3, 1), ("r1", 3, 0), ("r1", 2, 0), ("r3", 1), ("r3", 0),
    ("r1", 2, 1), ("r2", 3, 0), ("r2", 3, 1), ("r4", 1), ("r4", 0), ("r2", 2, 0),
    ("r2", 2, 1), ("r3", 3), ("act", 1), ("r3", 2), ("act", 0), ("c1", 1),
    ("ta", 0), ("r4", 3), ("r4", 2), ("c1", 0), ("c2", 1, 1), ("c2", 1, 0),
    ("ta", 1), ("act", 3), ("act", 2), ("c3", 1, 0), ("c2", 0, 0), ("c1", 3),
    ("c3", 1, 1), ("c1", 2), ("ta", 3), ("c2", 0, 1), ("c3", 0, 0), ("c2", 3, 0),
    ("ta", 2), ("c2", 2, 0), ("c2", 2, 1), ("c3", 0, 1), ("c2", 3, 1), ("p", 1),
    ("c3", 2, 1), ("c3", 2, 0), ("c3", 3, 0), ("c3", 3, 1), ("p", 0), ("m", 1),
    ("p", 2), ("m", 0), ("p", 3), ("m", 2), ("z", 1), ("z", 0),
    ("m", 3), ("z", 2), ("z", 3), ("g", 3), ("g", 2), ("g", 1),
    ("g", 0),
)


def slot_of(offset):
    return OFFSETS.index(4 if offset == -4 else offset)


def gelu_parts(preact):
    inner = tanh_scale * (preact + cubic_coeff * preact * preact * preact)
    hyper = jnp.tanh(inner)
    activated = 0.5 * preact * (1.0 + hyper)
    derivative = 0.5 * (1.0 + hyper) + 0.5 * preact * (1.0 - hyper * hyper) * tanh_scale * (
        1.0 + 3.0 * cubic_coeff * preact * preact
    )
    return (activated, derivative)


def contract(left, right, left_dim, right_dim):
    return lax.dot_general(
        left, right, (((left_dim,), (right_dim,)), ((), ())), preferred_element_type=jnp.float32
    )


def rows_of(value):
    return value.reshape((-1, value.shape[-1]))


def kernel(
    act_hbm, up_hbm, down_hbm, cot_hbm,
    out_hbm, in_grad_hbm, up_grad_hbm, down_grad_hbm,
    tok, act_t, w_up, w_down, acc0, s1, r1, acc2, s2, r2, acc3, s3, r3, acc4, s4, r4,
    hp, part, q0, ky, sy, ry, own, ds, rd, up_out, down_out, small_out,
    load_sem, store_sem, send_sem, recv_sem,
):
    bf16, f32 = jnp.bfloat16, jnp.float32
    width = tok.shape[-1]
    half = width // 2
    depth, row, z = lax.axis_index("depth"), lax.axis_index("row"), lax.axis_index("col")
    yl, k = depth // 2, depth % 2
    x, yh = row // 4, row % 4
    f1x, f2x = (x + x // 2) % 2, x // 2
    f1y, f2y = (yh + yh // 2) % 2, yh // 2
    def device(depth_at, row_at, col_at):
        return {"depth": depth_at, "row": row_at, "col": col_at}

    p1x = device(depth, (x + 1 - 2 * (x % 2)) * 4 + yh, z)
    p2x = device(depth, (3 - x) * 4 + yh, z)
    p1y = device(depth, x * 4 + yh + 1 - 2 * (yh % 2), z)
    p2y = device(depth, x * 4 + 3 - yh, z)
    sibling = device(yl * 2 + 1 - k, row, z)
    ypartner = device((1 - yl) * 2 + k, row, z)
    cols = {offset: device(depth, row, (z + offset + 8) % 8) for offset in OFFSETS[1:]}

    def along(offset):
        return cols[offset]

    partners = [sibling, ypartner, p1x, p2x, p1y, p2y] + [along(o) for o in OFFSETS[1:]]

    started, kinds = [], []

    def send(kind, src, dst, target):
        n = len(started)
        if kind not in kinds:
            kinds.append(kind)
        copy = pltpu.make_async_remote_copy(
            src_ref=src, dst_ref=dst, send_sem=send_sem.at[kinds.index(kind)],
            recv_sem=recv_sem.at[n], device_id=target,
            device_id_type=pl.DeviceIdType.MESH,
        )
        copy.start()
        started.append(copy)
        return copy

    loads = [
        pltpu.make_async_copy(act_hbm, tok.at[0, k, 0, yl], load_sem.at[0]),
        pltpu.make_async_copy(cot_hbm, tok.at[0, k, 1, yl], load_sem.at[1]),
        pltpu.make_async_copy(up_hbm, w_up, load_sem.at[2]),
        pltpu.make_async_copy(down_hbm, w_down, load_sem.at[3]),
    ]
    for load in loads:
        load.start()
    barrier = pltpu.get_barrier_semaphore()
    for target in partners:
        pl.semaphore_signal(
            barrier, inc=1, device_id=target, device_id_type=pl.DeviceIdType.MESH
        )
    pl.semaphore_wait(barrier, len(partners))

    flow, across, shared = {}, {}, {}

    def block(slot, a=slice(None)):
        return tok.at[slot, k, a, yl]

    def hop(offset, way, a=slice(None)):
        target = offset - way
        flow[target] = flow.get(target, []) + [
            send("hop", block(slot_of(offset), a), block(slot_of(target), a), along(way))
        ]

    def cross(slot):
        across[slot] = send("cross", block(slot), block(slot), ypartner)

    def arrive(offset):
        for copy in flow[offset]:
            copy.wait_recv()

    def share(c):
        for slot in (2 * c, 2 * c + 1):
            across[slot].wait_recv()
        mine = tok.at[2 * c : 2 * c + 2, k]
        shared[c] = send("share", mine, mine, sibling)

    wave, joined, widened = {}, [], []

    def flip_tokens(c):
        act_t[:, c * 8 * BLK : (c + 1) * 8 * BLK] = rows_of(tok[2 * c : 2 * c + 2, :, 0]).T

    def reduce1(c, a):
        if c not in joined:
            shared[c].wait_recv()
            joined.append(c)
        i, f = 2 * c + a, (f1x, f2x)[a]
        rows = rows_of(tok[2 * c : 2 * c + 2, :, a])
        value = contract(rows, (w_up, w_down)[a][...], 1, a)
        acc0[i] = value.reshape(acc0.shape[1:])
        s1[i] = (acc0[i, 1 - f] if a == 0 else acc0[i, :, 1 - f]).astype(bf16)
        wave[c, a] = send("s1", s1.at[i], r1.at[i], (p1x, p2x)[a])

    def reduce2(c, a):
        i, f, g = 2 * c + a, (f1x, f2x)[a], (f2x, f1x)[a]
        wave[c, a].wait_recv()

        def total(n):
            kept = acc0[i, f, n] if a == 0 else acc0[i, n, f]
            return kept + r1[i, n].astype(f32)

        value = total(1 - g).astype(bf16)
        s2[i, :, 0] = value[..., :half]
        s2[i, :, 1] = value[..., half:]
        wave[c, a] = send("s2", s2.at[i], r2.at[i], (p2x, p1x)[a])
        value = total(g)
        acc2[i, :, 0] = value[..., :half]
        acc2[i, :, 1] = value[..., half:]

    def reduce3(c):
        pair_of, f = slice(2 * c, 2 * c + 2), (f1y, f2y)[c % 2]
        wave[c, 0].wait_recv()
        wave[c, 1].wait_recv()

        def total(n):
            if c % 2 == 0:
                return acc2[pair_of, n] + r2[pair_of, n].astype(f32)
            return acc2[pair_of, :, n] + r2[pair_of, :, n].astype(f32)

        s3[pair_of] = total(1 - f).astype(bf16)
        wave[c] = send("s3", s3.at[pair_of], r3.at[pair_of], (p1y, p2y)[c % 2])
        acc3[pair_of] = total(f)

    def reduce4(c):
        pair_of, f = slice(2 * c, 2 * c + 2), (f2y, f1y)[c % 2]
        wave[c].wait_recv()
        s4[pair_of] = acc3[pair_of, 1 - f] + r3[pair_of, 1 - f].astype(f32)
        wave[c] = send("s4", s4.at[pair_of], r4.at[pair_of], (p2y, p1y)[c % 2])
        acc4[pair_of] = acc3[pair_of, f] + r3[pair_of, f].astype(f32)

    def activate(c):
        wave[c].wait_recv()
        activated, derivative = gelu_parts(acc4[2 * c] + r4[2 * c])
        backed = acc4[2 * c + 1] + r4[2 * c + 1]
        hp[c, 0, f1x, f2x, f1y, f2y] = activated.astype(bf16)
        hp[c, 1, f1x, f2x, f1y, f2y] = (backed * derivative).astype(bf16)
        region = hp.at[c, :, f1x, f2x, f1y, f2y]
        wave[c] = send("d0", region, region, (p2y, p1y)[c % 2])

    def double1(c):
        wave[c].wait_recv()
        region = hp.at[c, :, f1x, f2x, f1y] if c % 2 == 0 else hp.at[c, :, f1x, f2x, :, f2y]
        wave[c] = send("d1", region, region, (p1y, p2y)[c % 2])

    def double2(c, a):
        if c not in widened:
            wave[c].wait_recv()
            widened.append(c)
        region = hp.at[c, a, f1x, f2x]
        wave[c, a] = send("d2", region, region, (p2x, p1x)[a])

    def double3(c, a):
        wave[c, a].wait_recv()
        region = hp.at[c, a, f1x] if a == 0 else hp.at[c, a, :, f2x]
        wave[c, a] = send("d3", region, region, (p1x, p2x)[a])

    pair, cut, scattered = {}, {}, []

    def project(c):
        for a in range(2):
            wave[c, a].wait_recv()
            low, high = rows_of(hp[c, a, :, :, :, 0]), rows_of(hp[c, a, :, :, :, 1])
            rows = jnp.concatenate([low, high], axis=1)
            value = contract(rows, (w_down, w_up)[a][...], 1, a).reshape((2, 2, 2, BLK, width))
            part[c, 0, a] = value[:, 0]
            part[c, 1, a] = value[:, 1]
        pair[c] = send("part", part.at[c, 1 - k], q0.at[c], sibling)

    def merge(c):
        pair[c].wait_recv()
        sy[c] = (part[c, k, :, :, 1 - yl] + q0[c, :, :, 1 - yl]).astype(bf16)
        cut[c] = send("sy", sy.at[c], ry.at[c], ypartner)
        ky[c] = part[c, k, :, :, yl] + q0[c, :, :, yl]

    def scatter(c):
        cut[c].wait_recv()
        for s in (1, 0):
            slot = 2 * c + s
            value = ky[c, :, s] + ry[c, :, s].astype(f32)
            if slot == 0:
                own[...] = value
            else:
                ds[slot] = value.astype(bf16)
                scattered.append(send("ds", ds.at[slot], rd.at[slot], along(OFFSETS[slot])))

    stores = []

    def store(src, dst):
        stores.append(pltpu.make_async_copy(src, dst, store_sem.at[len(stores)]))
        stores[-1].start()

    def up_grad(h):
        cols = slice(h * half, (h + 1) * half)
        right = rows_of(hp[:, 1, :, :, :, h])
        up_out[:, cols] = contract(act_t[...], right, 1, 0).astype(bf16)
        store(up_out.at[:, cols], up_grad_hbm.at[:, cols])

    def down_grad(h):
        rows = slice(h * half, (h + 1) * half)
        left, right = rows_of(hp[:, 0, :, :, :, h]), rows_of(tok[:, :, 1])
        down_out[rows, :] = contract(left, right, 0, 0).astype(bf16)
        store(down_out.at[rows], down_grad_hbm.at[rows])

    def begin():
        loads[0].wait()
        loads[1].wait()
        hop(0, 1)
        hop(0, -1)
        cross(0)
        hop(0, 2)
        hop(0, -2)

    def pass_on(offset):
        arrive(offset)
        if offset == 4:
            arrive(-4)
        if offset in (2, -2):
            way = -offset // 2
            hop(offset, way)
            hop(offset, 2 * way, 0 if way == 1 else 1)
        cross(slot_of(offset))

    def grads(n):
        (up_grad, down_grad)[n // 2](n % 2)

    stages = {
        "y": pass_on, "s": share, "ta": flip_tokens, "r1": reduce1, "r2": reduce2,
        "r3": reduce3, "r4": reduce4, "act": activate, "c1": double1, "c2": double2,
        "c3": double3, "p": project, "m": merge, "z": scatter, "g": grads,
    }
    begin()
    loads[2].wait()
    loads[3].wait()
    for stage, *where in ORDER:
        stages[stage](*where)
    for copy in scattered:
        copy.wait_recv()
    for a, ref in ((0, out_hbm), (1, in_grad_hbm)):
        total = own[a]
        for slot in range(1, 8):
            total = total + rd[slot, a].astype(f32)
        small_out[a] = total.astype(bf16)
        store(small_out.at[a], ref)
    sent = {
        "hop": tok.at[0:7, 0, :, 0], "cross": tok.at[:, 0, :, 0], "share": tok.at[:, 0],
        "s1": s1, "s2": s2, "s3": s3, "s4": s4, "d0": hp.at[:, :, 0, 0, 0, 0],
        "d1": hp.at[:, :, 0, 0, 0], "d2": hp.at[:, :, 0, 0], "d3": hp.at[:, :, 0],
        "part": q0, "sy": sy, "ds": ds.at[1:8],
    }
    for kind, ref in sent.items():
        pltpu.make_async_copy(ref, ref, send_sem.at[kinds.index(kind)]).wait()
    for copy in stores:
        copy.wait()


KINDS, COPIES = 14, 96


def place(*refs):
    arrays, results, buffers, load_sem, store_sem = refs[:4], refs[4:8], refs[8:12], refs[12], refs[13]
    loads, stores = [], []
    for src, dst, buffer in zip(arrays, results, buffers):
        rows = src.shape[0]
        step = min(rows, 256)
        for first in range(0, rows, step):
            n, part = len(loads), pl.ds(first, step)
            loads.append(pltpu.make_async_copy(src.at[part], buffer.at[part], load_sem.at[n]))
            stores.append(pltpu.make_async_copy(buffer.at[part], dst.at[part], store_sem.at[n]))
    for load in loads:
        load.start()
    for load, store in zip(loads, stores):
        load.wait()
        store.start()
    for store in stores:
        store.wait()


def shards(activations, weight_up, weight_down, out_grad):
    width, hidden = weight_up.shape
    bf16, f32 = jnp.bfloat16, jnp.float32
    assert activations.shape[0] == BLK and width == hidden

    def vmem(lead, kind):
        return pltpu.VMEM(lead + (BLK, width), kind)

    def halves(lead, kind):
        return pltpu.VMEM(lead + (BLK, hidden // 2), kind)

    pieces = 2 * CHUNKS
    scratch = [
        vmem((8, 2, 2, 2), bf16),
        pltpu.VMEM((width, 8 * CHUNKS * BLK), bf16),
        pltpu.VMEM((width, hidden), bf16), pltpu.VMEM((width, hidden), bf16),
        vmem((pieces, 2, 2, 2), f32), vmem((pieces, 2, 2), bf16), vmem((pieces, 2, 2), bf16),
        halves((pieces, 2, 2), f32), halves((pieces, 2, 2), bf16), halves((pieces, 2, 2), bf16),
        halves((pieces, 2), f32), halves((pieces, 2), bf16), halves((pieces, 2), bf16),
        halves((pieces,), f32), halves((pieces,), f32), halves((pieces,), f32),
        halves((CHUNKS, 2, 2, 2, 2, 2), bf16),
        vmem((CHUNKS, 2, 2, 2, 2), f32), vmem((CHUNKS, 2, 2, 2), f32),
        vmem((CHUNKS, 2, 2), f32), vmem((CHUNKS, 2, 2), bf16), vmem((CHUNKS, 2, 2), bf16),
        vmem((2,), f32), vmem((8, 2), bf16), vmem((8, 2), bf16),
        pltpu.VMEM((width, hidden), bf16), pltpu.VMEM((width, hidden), bf16), vmem((2,), bf16),
        pltpu.SemaphoreType.DMA((4,)), pltpu.SemaphoreType.DMA((6,)),
        pltpu.SemaphoreType.DMA((KINDS,)), pltpu.SemaphoreType.DMA((COPIES,)),
    ]
    small = jax.ShapeDtypeStruct(activations.shape, bf16)
    large = jax.ShapeDtypeStruct(weight_up.shape, bf16)
    results = pl.pallas_call(
        kernel,
        out_shape=(small, small, large, large),
        in_specs=[pl.BlockSpec(memory_space=pltpu.HBM)] * 4,
        out_specs=[pl.BlockSpec(memory_space=pltpu.HBM)] * 4,
        scratch_shapes=scratch,
        compiler_params=pltpu.CompilerParams(
            collective_id=0, has_side_effects=True, vmem_limit_bytes=VMEM_MIB * 1024 * 1024
        ),
        cost_estimate=pl.CostEstimate(
            flops=12 * 512 * width * hidden, bytes_accessed=8 * width * hidden, transcendentals=0
        ),
        name="layer",
    )(activations, weight_up, weight_down, out_grad)
    out, in_grad, up_grad, down_grad = results
    up_grad, down_grad, out, in_grad = pl.pallas_call(
        place,
        out_shape=(large, large, small, small),
        in_specs=[pl.BlockSpec(memory_space=pltpu.HBM)] * 4,
        out_specs=[pl.BlockSpec(memory_space=pltpu.HBM)] * 4,
        scratch_shapes=[pltpu.VMEM(result.shape, bf16) for result in (large, large, small, small)]
        + [pltpu.SemaphoreType.DMA((8,)), pltpu.SemaphoreType.DMA((8,))],
        compiler_params=pltpu.CompilerParams(vmem_limit_bytes=VMEM_MIB * 1024 * 1024),
        name="place",
    )(up_grad, down_grad, out, in_grad)
    return out, in_grad, up_grad, down_grad


VMEM_MIB = 60


def solution(mesh):
    placed = (
        P(("depth", "col"), "row"),
        P("row", ("depth", "col")),
        P(("depth", "col"), "row"),
        P(("depth", "col"), "row"),
    )
    return jax.shard_map(
        shards,
        mesh=mesh,
        in_specs=placed,
        out_specs=(
            P(("depth", "col"), "row"),
            P(("depth", "col"), "row"),
            P("row", ("depth", "col")),
            P(("depth", "col"), "row"),
        ),
        check_vma=False,
    )
```

time: 87.9 us -> 90.9 us (1.034)
  Pallas kernels: 86.4 us -> 89.8 us
    pallas_call x1, Pallas kernels: 83.9 us -> 87.2 us  [shards(): pl.pallas_call(kernel, out_shape=(small, small, large, large), in_specs=[...]
where the time goes in v4:
time: 90.9 us; the launch traced here: 90.4 us
  Pallas kernels  89.8 us (99%)
    pallas_call x1, Pallas kernels, shards(): pl.pallas_call(kernel, out_shape=(small, small, large, large), in_specs=[...  87.2 us
    pallas_call x1, Pallas kernels, shards(): pl.pallas_call(place, out_shape=(large, large, small, small), in_specs=[p...  2.53 us

profile of v4, /device:TPU:6, one launch (start us, length us, event | category | flops | bytes accessed | tf_op | source)
XLA Modules:
  0.0 90.4 jit_solution(3575872880071215477)
XLA Ops:
  0.6 87.2 %layer.1 = (bf16[16,768]{1,0:T(8,128)(2,1)}, bf16[16,768]{1,0:T(8,128)(2,1)}, bf16[768,768]{1,0:T(8,128)(2,1)}, bf16[768,768]{1,0:T(8,128)(2,1)}) custom-call(bf16[16,768]{1,0:T(8,128)(2,1)} %act_hbm.1, bf16[768,768]{1,0:T(8,128)(2,1)} %up_hbm.1, bf16[768,768]{1,0:T(8,128)(2,1)} %down_hbm.1, bf16[16,768]{1,0:T(8,128)(2,1)} %cot_hbm.1), custom_call_target="tpu_custom_call" | custom-call | flops 3623878656 | bytes 4718592 | tf_op jit(solution)/shard_map/layer/pallas_call | solution.py:373
  87.9 2.5 %place.1 = (bf16[768,768]{1,0:T(8,128)(2,1)}, bf16[768,768]{1,0:T(8,128)(2,1)}, bf16[16,768]{1,0:T(8,128)(2,1)}, bf16[16,768]{1,0:T(8,128)(2,1)}) custom-call(bf16[768,768]{1,0:T(8,128)(2,1)} %get-tuple-element.12.refs_0_, bf16[768,768]{1,0:T(8,128)(2,1)} %get-tuple-element.13.refs_1_, bf16[16,768]{1,0:T(8,128)(2,1)} %get-tuple-element.14.refs_2_, ...), custom_call_target="tpu_custom_call" | custom-call | tf_op jit(solution)/shard_map/place/pallas_call | solution.py:388

commit v5 on v3

--- a/solution.py
+++ b/solution.py
@@ -10,6 +10,7 @@
 
 OFFSETS = (0, 1, -1, 2, -2, 3, -3, 4)
 CHUNKS = 4
+Y_FIRST = (2,)
 BLK = 16
 
 
@@ -81,14 +82,23 @@
     def along(offset):
         return {"col": (z + offset + 8) % 8}
 
+    x_first = (f1x, f2x, f1y, f2y), (p1x, p2x, p1y, p2y)
+    y_first = (f1y, f2y, f1x, f2x), (p1y, p2y, p1x, p2x)
+
+    def roles(c):
+        return y_first if c in Y_FIRST else x_first
+
     partners = [sibling, ypartner, p1x, p2x, p1y, p2y] + [along(o) for o in OFFSETS[1:]]
 
-    started = []
-
-    def send(src, dst, device):
+    started, kinds = [], []
+
+    def send(kind, src, dst, device):
         n = len(started)
+        if kind not in kinds:
+            kinds.append(kind)
         copy = pltpu.make_async_remote_copy(
-            src_ref=src, dst_ref=dst, send_sem=send_sem.at[n], recv_sem=recv_sem.at[n],
+            src_ref=src, dst_ref=dst, send_sem=send_sem.at[kinds.index(kind)],
+            recv_sem=recv_sem.at[n],
             device_id=device, device_id_type=pl.DeviceIdType.MESH,
         )
         copy.start()
@@ -116,11 +126,11 @@
     def hop(offset, way, a=slice(None)):
         target = offset - way
         flow[target] = flow.get(target, []) + [
-            send(block(slot_of(offset), a), block(slot_of(target), a), along(way))
+            send("hop", block(slot_of(offset), a), block(slot_of(target), a), along(way))
         ]
 
     def cross(slot):
-        across[slot] = send(block(slot), block(slot), ypartner)
+        across[slot] = send("cross", block(slot), block(slot), ypartner)
 
     def arrive(offset):
         for copy in flow[offset]:
@@ -129,7 +139,7 @@
     def share(slot):
         across[slot].wait_recv()
         mine = tok.at[:, slot, k]
-        shared[slot] = send(mine, mine, sibling)
+        shared[slot] = send("share", mine, mine, sibling)
 
     wave, joined = {}, []
 
@@ -147,15 +157,17 @@
             if slot not in joined:
                 shared[slot].wait_recv()
                 joined.append(slot)
-        i, f = 2 * c + a, (f1x, f2x)[a]
+        (b1, b2, _, _), (p1, p2, _, _) = roles(c)
+        i, f = 2 * c + a, (b1, b2)[a]
         rows = rows_of(tok[a, 2 * c : 2 * c + 2])
         value = contract(rows, (w_up, w_down_t)[a][...], 1, 0)
         acc0[i] = value.reshape(acc0.shape[1:])
         s1[i] = (acc0[i, 1 - f] if a == 0 else acc0[i, :, 1 - f]).astype(bf16)
-        wave[c, a] = send(s1.at[i], r1.at[i], (p1x, p2x)[a])
+        wave[c, a] = send("s1", s1.at[i], r1.at[i], (p1, p2)[a])
 
     def reduce2(c, a):
-        i, f, g = 2 * c + a, (f1x, f2x)[a], (f2x, f1x)[a]
+        (b1, b2, _, _), (p1, p2, _, _) = roles(c)
+        i, f, g = 2 * c + a, (b1, b2)[a], (b2, b1)[a]
         wave[c, a].wait_recv()
 
         def total(n):
@@ -165,13 +177,14 @@
         value = total(1 - g).astype(bf16)
         s2[i, :, 0] = value[..., :half]
         s2[i, :, 1] = value[..., half:]
-        wave[c, a] = send(s2.at[i], r2.at[i], (p2x, p1x)[a])
+        wave[c, a] = send("s2", s2.at[i], r2.at[i], (p2, p1)[a])
         value = total(g)
         acc2[i, :, 0] = value[..., :half]
         acc2[i, :, 1] = value[..., half:]
 
     def reduce3(c, a):
-        i, f = 2 * c + a, (f1y, f2y)[a]
+        (_, _, b3, b4), (_, _, p3, p4) = roles(c)
+        i, f = 2 * c + a, (b3, b4)[a]
         wave[c, a].wait_recv()
 
         def total(n):
@@ -180,39 +193,42 @@
             return acc2[i, :, n] + r2[i, :, n].astype(f32)
 
         s3[i] = total(1 - f).astype(bf16)
-        wave[c, a] = send(s3.at[i], r3.at[i], (p1y, p2y)[a])
+        wave[c, a] = send("s3", s3.at[i], r3.at[i], (p3, p4)[a])
         acc3[i] = total(f)
 
     def reduce4(c, a):
-        i, f = 2 * c + a, (f2y, f1y)[a]
+        (_, _, b3, b4), (_, _, p3, p4) = roles(c)
+        i, f = 2 * c + a, (b4, b3)[a]
         wave[c, a].wait_recv()
         s4[i] = acc3[i, 1 - f] + r3[i, 1 - f].astype(f32)
-        wave[c, a] = send(s4.at[i], r4.at[i], (p2y, p1y)[a])
+        wave[c, a] = send("s4", s4.at[i], r4.at[i], (p4, p3)[a])
         acc4[i] = acc3[i, f] + r3[i, f].astype(f32)
 
     def double(c, a, step):
         if step > 0:
             wave[c, a].wait_recv()
+        (b1, b2, b3, b4), (p1, p2, p3, p4) = roles(c)
         if step == 0:
-            region, device = hp.at[c, a, f1x, f2x, f1y, f2y], (p2y, p1y)[a]
+            region, device = hp.at[c, a, b1, b2, b3, b4], (p4, p3)[a]
         elif step == 1:
-            region = hp.at[c, a, f1x, f2x, f1y] if a == 0 else hp.at[c, a, f1x, f2x, :, f2y]
-            device = (p1y, p2y)[a]
+            region = hp.at[c, a, b1, b2, b3] if a == 0 else hp.at[c, a, b1, b2, :, b4]
+            device = (p3, p4)[a]
         elif step == 2:
-            region, device = hp.at[c, a, f1x, f2x], (p2x, p1x)[a]
+            region, device = hp.at[c, a, b1, b2], (p2, p1)[a]
         else:
-            region = hp.at[c, a, f1x] if a == 0 else hp.at[c, a, :, f2x]
-            device = (p1x, p2x)[a]
-        wave[c, a] = send(region, region, device)
+            region = hp.at[c, a, b1] if a == 0 else hp.at[c, a, :, b2]
+            device = (p1, p2)[a]
+        wave[c, a] = send(("d0", "d1", "d2", "d3")[step], region, region, device)
 
     def activate(c):
         wave[c, 0].wait_recv()
         wave[c, 1].wait_recv()
+        b1, b2, b3, b4 = roles(c)[0]
         activated, derivative = gelu_parts(acc4[2 * c] + r4[2 * c])
-        hp[c, 0, f1x, f2x, f1y, f2y] = activated.astype(bf16)
+        hp[c, 0, b1, b2, b3, b4] = activated.astype(bf16)
         double(c, 0, 0)
         backed = acc4[2 * c + 1] + r4[2 * c + 1]
-        hp[c, 1, f1x, f2x, f1y, f2y] = (backed * derivative).astype(bf16)
+        hp[c, 1, b1, b2, b3, b4] = (backed * derivative).astype(bf16)
         double(c, 1, 0)
 
     pair, cut, scattered = {}, {}, []
@@ -223,12 +239,12 @@
         rows = jnp.concatenate([low, high], axis=1)
         value = contract(rows, (w_down, w_up_t)[a][...], 1, 0)
         part[c, a] = value.reshape(part.shape[2:])
-        pair[c, a] = send(part.at[c, a, :, 1 - k], q0.at[c, a], sibling)
+        pair[c, a] = send("part", part.at[c, a, :, 1 - k], q0.at[c, a], sibling)
 
     def merge(c, a):
         pair[c, a].wait_recv()
         sy[c, a] = (part[c, a, :, k, 1 - yl] + q0[c, a, :, 1 - yl]).astype(bf16)
-        cut[c, a] = send(sy.at[c, a], ry.at[c, a], ypartner)
+        cut[c, a] = send("sy", sy.at[c, a], ry.at[c, a], ypartner)
         ky[c, a] = part[c, a, :, k, yl] + q0[c, a, :, yl]
 
     def scatter(c):
@@ -241,7 +257,7 @@
                 own[...] = value
             else:
                 ds[slot] = value.astype(bf16)
-                scattered.append(send(ds.at[slot], rd.at[slot], along(OFFSETS[slot])))
+                scattered.append(send("ds", ds.at[slot], rd.at[slot], along(OFFSETS[slot])))
 
     stores = []
 
@@ -302,13 +318,19 @@
             total = total + rd[slot, a].astype(f32)
         small_out[a] = total.astype(bf16)
         store(small_out.at[a], ref)
-    for copy in started:
-        copy.wait_send()
+    sent = {
+        "hop": tok.at[:, 0:7, 0, 0], "cross": tok.at[:, :, 0, 0], "share": tok.at[:, :, 0],
+        "s1": s1, "s2": s2, "s3": s3, "s4": s4, "d0": hp.at[:, :, 0, 0, 0, 0],
+        "d1": hp.at[:, :, 0, 0, 0], "d2": hp.at[:, :, 0, 0], "d3": hp.at[:, :, 0],
+        "part": q0, "sy": sy, "ds": ds.at[1:8],
+    }
+    for kind, ref in sent.items():
+        pltpu.make_async_copy(ref, ref, send_sem.at[kinds.index(kind)]).wait()
     for copy in stores:
         copy.wait()
 
 
-COPIES = 128
+KINDS, COPIES = 14, 128
 
 
 def place(*refs):
@@ -357,8 +379,7 @@
         vmem((2,), f32), vmem((8, 2), bf16), vmem((8, 2), bf16),
         pltpu.VMEM((width, hidden), bf16), pltpu.VMEM((width, hidden), bf16), vmem((2,), bf16),
         pltpu.SemaphoreType.DMA((4,)), pltpu.SemaphoreType.DMA((6,)),
-        pltpu.SemaphoreType.DMA((COPIES,)),
-        pltpu.SemaphoreType.DMA((COPIES,)),
+        pltpu.SemaphoreType.DMA((KINDS,)), pltpu.SemaphoreType.DMA((COPIES,)),
     ]
     small = jax.ShapeDtypeStruct(activations.shape, bf16)
     large = jax.ShapeDtypeStruct(weight_up.shape, bf16)

time: 87.9 us -> 94.2 us (1.072)
  the two profiles are of different devices: /device:TPU:6 before, /device:TPU:1 now
where the time goes in v5:
time: 94.2 us; the launch traced here: 94 us
  Pallas kernels  93.4 us (99%)
    pallas_call x1, Pallas kernels, shards(): pl.pallas_call(kernel, out_shape=(small, small, large, large), in_specs=[...  90.8 us
    pallas_call x1, Pallas kernels, shards(): pl.pallas_call(place, out_shape=(large, large, small, small), in_specs=[p...  2.53 us

profile of v5, /device:TPU:1, one launch (start us, length us, event | category | flops | bytes accessed | tf_op | source)
XLA Modules:
  0.0 94.0 jit_solution(18175733862703579604)
XLA Ops:
  0.6 90.8 %layer.1 = (bf16[16,768]{1,0:T(8,128)(2,1)}, bf16[16,768]{1,0:T(8,128)(2,1)}, bf16[768,768]{1,0:T(8,128)(2,1)}, bf16[768,768]{1,0:T(8,128)(2,1)}) custom-call(bf16[16,768]{1,0:T(8,128)(2,1)} %act_hbm.1, bf16[768,768]{1,0:T(8,128)(2,1)} %up_hbm.1, bf16[768,768]{1,0:T(8,128)(2,1)} %down_hbm.1, bf16[16,768]{1,0:T(8,128)(2,1)} %cot_hbm.1), custom_call_target="tpu_custom_call" | custom-call | flops 3623878656 | bytes 4718592 | tf_op jit(solution)/shard_map/layer/pallas_call | solution.py:386
  91.5 2.5 %place.1 = (bf16[768,768]{1,0:T(8,128)(2,1)}, bf16[768,768]{1,0:T(8,128)(2,1)}, bf16[16,768]{1,0:T(8,128)(2,1)}, bf16[16,768]{1,0:T(8,128)(2,1)}) custom-call(bf16[768,768]{1,0:T(8,128)(2,1)} %get-tuple-element.12.refs_0_, bf16[768,768]{1,0:T(8,128)(2,1)} %get-tuple-element.13.refs_1_, bf16[16,768]{1,0:T(8,128)(2,1)} %get-tuple-element.14.refs_2_, ...), custom_call_target="tpu_custom_call" | custom-call | tf_op jit(solution)/shard_map/place/pallas_call | solution.py:401

commit v6 on v2

--- a/solution.py
+++ b/solution.py
@@ -18,11 +18,12 @@
     ("r1", 0), ("s", 3), ("y", 3), ("r1", 1), ("y", 4), ("y", -3), ("s", 4),
     ("s", 5), ("r2", 0), ("r1", 2), ("s", 6), ("s", 7), ("r2", 1), ("r3", 0),
     ("r1", 3), ("r2", 2), ("r3", 1), ("r4", 0), ("r2", 3), ("r3", 2), ("r4", 1),
-    ("r3", 3), ("r4", 2), ("act", 1), ("r4", 3), ("act", 2), ("c1", 1), ("act", 0),
-    ("c1", 2), ("c2", 1), ("act", 3), ("c2", 2), ("c3", 1), ("c1", 3), ("c3", 2),
-    ("c1", 0), ("c2", 3), ("p", 1), ("c2", 0), ("p", 2), ("c3", 3), ("m", 1),
-    ("c3", 0), ("m", 2), ("p", 3), ("z", 1), ("p", 0), ("z", 2), ("m", 3),
-    ("g", 3), ("g", 1), ("m", 0), ("z", 3), ("g", 0), ("g", 2), ("z", 0),
+    ("r3", 3), ("r4", 2), ("ta", 0), ("act", 1), ("r4", 3), ("act", 2), ("ta", 1),
+    ("c1", 1), ("act", 0), ("c1", 2), ("c2", 1), ("ta", 2), ("act", 3), ("c2", 2),
+    ("c3", 1), ("ta", 3), ("c1", 3), ("c3", 2), ("c1", 0), ("c2", 3), ("p", 1),
+    ("c2", 0), ("p", 2), ("c3", 3), ("m", 1), ("c3", 0), ("m", 2), ("p", 3),
+    ("z", 1), ("p", 0), ("z", 2), ("m", 3), ("m", 0), ("z", 3), ("z", 0),
+    ("g", 0), ("g", 1), ("g", 2), ("g", 3),
 )
 
 
@@ -53,7 +54,7 @@
 def kernel(
     act_hbm, up_hbm, down_hbm, cot_hbm,
     out_hbm, in_grad_hbm, up_grad_hbm, down_grad_hbm,
-    tok, w_up, w_down, acc0, s1, r1, acc2, s2, r2, acc3, s3, r3, acc4, s4, r4,
+    tok, act_t, w_up, w_down, acc0, s1, r1, acc2, s2, r2, acc3, s3, r3, acc4, s4, r4,
     hp, part, q0, ky, sy, ry, own, ds, rd, up_out, down_out, small_out,
     load_sem, store_sem, send_sem, recv_sem,
 ):
@@ -74,12 +75,15 @@
 
     partners = [sibling, ypartner, p1x, p2x, p1y, p2y] + [along(o) for o in OFFSETS[1:]]
 
-    started = []
-
-    def send(src, dst, device):
+    started, kinds = [], []
+
+    def send(kind, src, dst, device):
         n = len(started)
+        if kind not in kinds:
+            kinds.append(kind)
         copy = pltpu.make_async_remote_copy(
-            src_ref=src, dst_ref=dst, send_sem=send_sem.at[n], recv_sem=recv_sem.at[n],
+            src_ref=src, dst_ref=dst, send_sem=send_sem.at[kinds.index(kind)],
+            recv_sem=recv_sem.at[n],
             device_id=device, device_id_type=pl.DeviceIdType.MESH,
         )
         copy.start()
@@ -107,11 +111,11 @@
     def hop(offset, way, a=slice(None)):
         target = offset - way
         flow[target] = flow.get(target, []) + [
-            send(block(slot_of(offset), a), block(slot_of(target), a), along(way))
+            send("hop", block(slot_of(offset), a), block(slot_of(target), a), along(way))
         ]
 
     def cross(slot):
-        across[slot] = send(block(slot), block(slot), ypartner)
+        across[slot] = send("cross", block(slot), block(slot), ypartner)
 
     def arrive(offset):
         for copy in flow[offset]:
@@ -120,9 +124,12 @@
     def share(slot):
         across[slot].wait_recv()
         mine = tok.at[:, slot, k]
-        shared[slot] = send(mine, mine, sibling)
+        shared[slot] = send("share", mine, mine, sibling)
 
     wave = {}
+
+    def flip_tokens(c):
+        act_t[:, c * 8 * BLK : (c + 1) * 8 * BLK] = rows_of(tok[0, 2 * c : 2 * c + 2]).T
 
     def reduce1(c):
         for slot in (2 * c, 2 * c + 1):
@@ -133,7 +140,7 @@
             value = contract(rows, w_up[...], 1, 0) if a == 0 else contract(rows, w_down[...], 1, 1)
             acc0[i] = value.reshape(acc0.shape[1:])
             s1[i] = (acc0[i, 1 - f] if a == 0 else acc0[i, :, 1 - f]).astype(bf16)
-            wave[c, a] = send(s1.at[i], r1.at[i], (p1x, p2x)[a])
+            wave[c, a] = send("s1", s1.at[i], r1.at[i], (p1x, p2x)[a])
 
     def reduce2(c):
         for a in range(2):
@@ -147,7 +154,7 @@
             value = total(1 - g).astype(bf16)
             s2[i, :, 0] = value[..., :half]
             s2[i, :, 1] = value[..., half:]
-            wave[c, a] = send(s2.at[i], r2.at[i], (p2x, p1x)[a])
+            wave[c, a] = send("s2", s2.at[i], r2.at[i], (p2x, p1x)[a])
             value = total(g)
             acc2[i, :, 0] = value[..., :half]
             acc2[i, :, 1] = value[..., half:]
@@ -163,7 +170,7 @@
                 return acc2[i, :, n] + r2[i, :, n].astype(f32)
 
             s3[i] = total(1 - f).astype(bf16)
-            wave[c, a] = send(s3.at[i], r3.at[i], (p1y, p2y)[a])
+            wave[c, a] = send("s3", s3.at[i], r3.at[i], (p1y, p2y)[a])
             acc3[i] = total(f)
 
     def reduce4(c):
@@ -171,7 +178,7 @@
             i, f = 2 * c + a, (f2y, f1y)[a]
             wave[c, a].wait_recv()
             s4[i] = acc3[i, 1 - f] + r3[i, 1 - f].astype(f32)
-            wave[c, a] = send(s4.at[i], r4.at[i], (p2y, p1y)[a])
+            wave[c, a] = send("s4", s4.at[i], r4.at[i], (p2y, p1y)[a])
             acc4[i] = acc3[i, f] + r3[i, f].astype(f32)
 
     def double(c, step):
@@ -188,7 +195,7 @@
             else:
                 region = hp.at[c, a, f1x] if a == 0 else hp.at[c, a, :, f2x]
                 device = (p1x, p2x)[a]
-            wave[c, a] = send(region, region, device)
+            wave[c, a] = send(("d0", "d1", "d2", "d3")[step], region, region, device)
 
     def activate(c):
         wave[c, 0].wait_recv()
@@ -208,13 +215,13 @@
             rows = jnp.concatenate([low, high], axis=1)
             value = contract(rows, w_down[...], 1, 0) if a == 0 else contract(rows, w_up[...], 1, 1)
             part[c, a] = value.reshape(part.shape[2:])
-            pair[c, a] = send(part.at[c, a, :, 1 - k], q0.at[c, a], sibling)
+            pair[c, a] = send("part", part.at[c, a, :, 1 - k], q0.at[c, a], sibling)
 
     def merge(c):
         for a in range(2):
             pair[c, a].wait_recv()
             sy[c, a] = (part[c, a, :, k, 1 - yl] + q0[c, a, :, 1 - yl]).astype(bf16)
-        cut[c] = send(sy.at[c], ry.at[c], ypartner)
+        cut[c] = send("sy", sy.at[c], ry.at[c], ypartner)
         for a in range(2):
             ky[c, a] = part[c, a, :, k, yl] + q0[c, a, :, yl]
 
@@ -227,7 +234,7 @@
                 own[...] = value
             else:
                 ds[slot] = value.astype(bf16)
-                scattered.append(send(ds.at[slot], rd.at[slot], along(OFFSETS[slot])))
+                scattered.append(send("ds", ds.at[slot], rd.at[slot], along(OFFSETS[slot])))
 
     stores = []
 
@@ -237,8 +244,8 @@
 
     def up_grad(h):
         cols = slice(h * half, (h + 1) * half)
-        left, right = rows_of(tok[0]), rows_of(hp[:, 1, :, :, :, h])
-        up_out[:, cols] = contract(left, right, 0, 0).astype(bf16)
+        right = rows_of(hp[:, 1, :, :, :, h])
+        up_out[:, cols] = contract(act_t[...], right, 1, 0).astype(bf16)
         store(up_out.at[:, cols], up_grad_hbm.at[:, cols])
 
     def down_grad(h):
@@ -270,7 +277,7 @@
         (up_grad, down_grad)[n // 2](n % 2)
 
     stages = {
-        "y": pass_on, "s": share, "r1": reduce1, "r2": reduce2, "r3": reduce3, "r4": reduce4,
+        "y": pass_on, "s": share, "ta": flip_tokens, "r1": reduce1, "r2": reduce2, "r3": reduce3, "r4": reduce4,
         "act": activate, "c1": lambda c: double(c, 1), "c2": lambda c: double(c, 2),
         "c3": lambda c: double(c, 3), "p": project, "m": merge, "z": scatter, "g": grads,
     }
@@ -287,13 +294,19 @@
             total = total + rd[slot, a].astype(f32)
         small_out[a] = total.astype(bf16)
         store(small_out.at[a], ref)
-    for copy in started:
-        copy.wait_send()
+    sent = {
+        "hop": tok.at[:, 0:7, 0, 0], "cross": tok.at[:, :, 0, 0], "share": tok.at[:, :, 0],
+        "s1": s1, "s2": s2, "s3": s3, "s4": s4, "d0": hp.at[:, :, 0, 0, 0, 0],
+        "d1": hp.at[:, :, 0, 0, 0], "d2": hp.at[:, :, 0, 0], "d3": hp.at[:, :, 0],
+        "part": q0, "sy": sy, "ds": ds.at[1:8],
+    }
+    for kind, ref in sent.items():
+        pltpu.make_async_copy(ref, ref, send_sem.at[kinds.index(kind)]).wait()
     for copy in stores:
         copy.wait()
 
 
-COPIES = 128
+KINDS, COPIES = 14, 128
 
 
 def place(*refs):
@@ -329,6 +342,7 @@
     pieces = 2 * CHUNKS
     scratch = [
         vmem((2, 8, 2, 2), bf16),
+        pltpu.VMEM((width, 8 * CHUNKS * BLK), bf16),
         pltpu.VMEM((width, hidden), bf16), pltpu.VMEM((width, hidden), bf16),
         vmem((pieces, 2, 2, 2), f32), vmem((pieces, 2, 2), bf16), vmem((pieces, 2, 2), bf16),
         halves((pieces, 2, 2), f32), halves((pieces, 2, 2), bf16), halves((pieces, 2, 2), bf16),
@@ -340,8 +354,7 @@
         vmem((2,), f32), vmem((8, 2), bf16), vmem((8, 2), bf16),
         pltpu.VMEM((width, hidden), bf16), pltpu.VMEM((width, hidden), bf16), vmem((2,), bf16),
         pltpu.SemaphoreType.DMA((4,)), pltpu.SemaphoreType.DMA((6,)),
-        pltpu.SemaphoreType.DMA((COPIES,)),
-        pltpu.SemaphoreType.DMA((COPIES,)),
+        pltpu.SemaphoreType.DMA((KINDS,)), pltpu.SemaphoreType.DMA((COPIES,)),
     ]
     small = jax.ShapeDtypeStruct(activations.shape, bf16)
     large = jax.ShapeDtypeStruct(weight_up.shape, bf16)

time: 86.5 us -> 86.6 us (level)
  no operation moved by 1% of the time
where the time goes in v6:
time: 86.6 us; the launch traced here: 86.1 us
  Pallas kernels  85.5 us (99%)
    pallas_call x1, Pallas kernels, shards(): pl.pallas_call(kernel, out_shape=(small, small, large, large), in_specs=[...  82.9 us
    pallas_call x1, Pallas kernels, shards(): pl.pallas_call(place, out_shape=(large, large, small, small), in_specs=[p...  2.53 us

profile of v6, /device:TPU:6, one launch (start us, length us, event | category | flops | bytes accessed | tf_op | source)
XLA Modules:
  0.0 86.1 jit_solution(11207536197056356373)
XLA Ops:
  0.6 82.9 %layer.1 = (bf16[16,768]{1,0:T(8,128)(2,1)}, bf16[16,768]{1,0:T(8,128)(2,1)}, bf16[768,768]{1,0:T(8,128)(2,1)}, bf16[768,768]{1,0:T(8,128)(2,1)}) custom-call(bf16[16,768]{1,0:T(8,128)(2,1)} %act_hbm.1, bf16[768,768]{1,0:T(8,128)(2,1)} %up_hbm.1, bf16[768,768]{1,0:T(8,128)(2,1)} %down_hbm.1, bf16[16,768]{1,0:T(8,128)(2,1)} %cot_hbm.1), custom_call_target="tpu_custom_call" | custom-call | flops 3623878656 | bytes 4718592 | tf_op jit(solution)/shard_map/layer/pallas_call | solution.py:361
  83.6 2.5 %place.1 = (bf16[768,768]{1,0:T(8,128)(2,1)}, bf16[768,768]{1,0:T(8,128)(2,1)}, bf16[16,768]{1,0:T(8,128)(2,1)}, bf16[16,768]{1,0:T(8,128)(2,1)}) custom-call(bf16[768,768]{1,0:T(8,128)(2,1)} %get-tuple-element.12.refs_0_, bf16[768,768]{1,0:T(8,128)(2,1)} %get-tuple-element.13.refs_1_, bf16[16,768]{1,0:T(8,128)(2,1)} %get-tuple-element.14.refs_2_, ...), custom_call_target="tpu_custom_call" | custom-call | tf_op jit(solution)/shard_map/place/pallas_call | solution.py:376

commit v7 on v6

--- a/solution.py
+++ b/solution.py
@@ -14,9 +14,9 @@
 
 
 ORDER = (
-    ("y", 1), ("s", 0), ("y", -1), ("s", 1), ("y", 2), ("y", -2), ("s", 2),
-    ("r1", 0), ("s", 3), ("y", 3), ("r1", 1), ("y", 4), ("y", -3), ("s", 4),
-    ("s", 5), ("r2", 0), ("r1", 2), ("s", 6), ("s", 7), ("r2", 1), ("r3", 0),
+    ("y", 1), ("y", -1), ("s", 0), ("s", 1), ("s", 2), ("y", 2), ("y", -2),
+    ("r1", 0), ("s", 3), ("s", 4), ("y", 3), ("y", -3), ("r1", 1), ("s", 5),
+    ("s", 6), ("y", 4), ("s", 7), ("r2", 0), ("r1", 2), ("r2", 1), ("r3", 0),
     ("r1", 3), ("r2", 2), ("r3", 1), ("r4", 0), ("r2", 3), ("r3", 2), ("r4", 1),
     ("r3", 3), ("r4", 2), ("ta", 0), ("act", 1), ("r4", 3), ("act", 2), ("ta", 1),
     ("c1", 1), ("act", 0), ("c1", 2), ("c2", 1), ("ta", 2), ("act", 3), ("c2", 2),
@@ -103,28 +103,17 @@
         pl.semaphore_signal(barrier, inc=1, device_id=device, device_id_type=pl.DeviceIdType.MESH)
     pl.semaphore_wait(barrier, len(partners))
 
-    flow, across, shared = {}, {}, {}
-
-    def block(slot, a=slice(None)):
-        return tok.at[a, slot, k, yl]
+    flow, shared = {}, {}
+
+    def slab(slot, a=slice(None)):
+        return tok.at[a, slot, k]
 
     def hop(offset, way, a=slice(None)):
         target = offset - way
-        flow[target] = flow.get(target, []) + [
-            send("hop", block(slot_of(offset), a), block(slot_of(target), a), along(way))
-        ]
-
-    def cross(slot):
-        across[slot] = send("cross", block(slot), block(slot), ypartner)
-
-    def arrive(offset):
-        for copy in flow[offset]:
-            copy.wait_recv()
+        flow[target] = send("hop", slab(slot_of(offset), a), slab(slot_of(target), a), along(way))
 
     def share(slot):
-        across[slot].wait_recv()
-        mine = tok.at[:, slot, k]
-        shared[slot] = send("share", mine, mine, sibling)
+        shared[slot] = send("share", slab(slot), slab(slot), sibling)
 
     wave = {}
 
@@ -257,21 +246,18 @@
     def begin():
         loads[0].wait()
         loads[1].wait()
+        mine = tok.at[:, 0, k, yl]
+        send("cross", mine, mine, ypartner).wait_recv()
         hop(0, 1)
         hop(0, -1)
-        cross(0)
-        hop(0, 2)
-        hop(0, -2)
 
     def pass_on(offset):
-        arrive(offset)
+        flow[offset].wait_recv()
         if offset == 4:
-            arrive(-4)
-        if offset in (2, -2):
-            way = -offset // 2
-            hop(offset, way)
-            hop(offset, 2 * way, 0 if way == 1 else 1)
-        cross(slot_of(offset))
+            flow[-4].wait_recv()
+        else:
+            way = -1 if offset > 0 else 1
+            hop(offset, way, slice(None) if abs(offset) < 3 else (0 if way == 1 else 1))
 
     def grads(n):
         (up_grad, down_grad)[n // 2](n % 2)
@@ -295,7 +281,7 @@
         small_out[a] = total.astype(bf16)
         store(small_out.at[a], ref)
     sent = {
-        "hop": tok.at[:, 0:7, 0, 0], "cross": tok.at[:, :, 0, 0], "share": tok.at[:, :, 0],
+        "hop": tok.at[:, 0:7, 0], "cross": tok.at[:, 0, 0, 0], "share": tok.at[:, :, 0],
         "s1": s1, "s2": s2, "s3": s3, "s4": s4, "d0": hp.at[:, :, 0, 0, 0, 0],
         "d1": hp.at[:, :, 0, 0, 0], "d2": hp.at[:, :, 0, 0], "d3": hp.at[:, :, 0],
         "part": q0, "sy": sy, "ds": ds.at[1:8],

time: 86.6 us -> 90.2 us (1.042)
  Pallas kernels: 85.5 us -> 88.5 us
    pallas_call x1, Pallas kernels: 82.9 us -> 86 us  [shards(): pl.pallas_call(kernel, out_shape=(small, small, large, large), in_specs=[...]
where the time goes in v7:
time: 90.2 us; the launch traced here: 89.1 us
  Pallas kernels  88.5 us (98%)
    pallas_call x1, Pallas kernels, shards(): pl.pallas_call(kernel, out_shape=(small, small, large, large), in_specs=[...  86 us
    pallas_call x1, Pallas kernels, shards(): pl.pallas_call(place, out_shape=(large, large, small, small), in_specs=[p...  2.53 us

profile of v7, /device:TPU:6, one launch (start us, length us, event | category | flops | bytes accessed | tf_op | source)
XLA Modules:
  0.0 89.1 jit_solution(7584857534436778117)
XLA Ops:
  0.6 86.0 %layer.1 = (bf16[16,768]{1,0:T(8,128)(2,1)}, bf16[16,768]{1,0:T(8,128)(2,1)}, bf16[768,768]{1,0:T(8,128)(2,1)}, bf16[768,768]{1,0:T(8,128)(2,1)}) custom-call(bf16[16,768]{1,0:T(8,128)(2,1)} %act_hbm.1, bf16[768,768]{1,0:T(8,128)(2,1)} %up_hbm.1, bf16[768,768]{1,0:T(8,128)(2,1)} %down_hbm.1, bf16[16,768]{1,0:T(8,128)(2,1)} %cot_hbm.1), custom_call_target="tpu_custom_call" | custom-call | flops 3623878656 | bytes 4718592 | tf_op jit(solution)/shard_map/layer/pallas_call | solution.py:347
  86.6 2.5 %place.1 = (bf16[768,768]{1,0:T(8,128)(2,1)}, bf16[768,768]{1,0:T(8,128)(2,1)}, bf16[16,768]{1,0:T(8,128)(2,1)}, bf16[16,768]{1,0:T(8,128)(2,1)}) custom-call(bf16[768,768]{1,0:T(8,128)(2,1)} %get-tuple-element.12.refs_0_, bf16[768,768]{1,0:T(8,128)(2,1)} %get-tuple-element.13.refs_1_, bf16[16,768]{1,0:T(8,128)(2,1)} %get-tuple-element.14.refs_2_, ...), custom_call_target="tpu_custom_call" | custom-call | tf_op jit(solution)/shard_map/place/pallas_call | solution.py:362

commit v8 on v6

--- a/solution.py
+++ b/solution.py
@@ -14,16 +14,15 @@
 
 
 ORDER = (
-    ("y", 1), ("s", 0), ("y", -1), ("s", 1), ("y", 2), ("y", -2), ("s", 2),
-    ("r1", 0), ("s", 3), ("y", 3), ("r1", 1), ("y", 4), ("y", -3), ("s", 4),
-    ("s", 5), ("r2", 0), ("r1", 2), ("s", 6), ("s", 7), ("r2", 1), ("r3", 0),
-    ("r1", 3), ("r2", 2), ("r3", 1), ("r4", 0), ("r2", 3), ("r3", 2), ("r4", 1),
-    ("r3", 3), ("r4", 2), ("ta", 0), ("act", 1), ("r4", 3), ("act", 2), ("ta", 1),
-    ("c1", 1), ("act", 0), ("c1", 2), ("c2", 1), ("ta", 2), ("act", 3), ("c2", 2),
-    ("c3", 1), ("ta", 3), ("c1", 3), ("c3", 2), ("c1", 0), ("c2", 3), ("p", 1),
-    ("c2", 0), ("p", 2), ("c3", 3), ("m", 1), ("c3", 0), ("m", 2), ("p", 3),
-    ("z", 1), ("p", 0), ("z", 2), ("m", 3), ("m", 0), ("z", 3), ("z", 0),
-    ("g", 0), ("g", 1), ("g", 2), ("g", 3),
+    ("y", 1), ("y", -1), ("s", 0), ("y", 2), ("y", -2), ("r1", 0), ("s", 1),
+    ("y", 3), ("r1", 1), ("y", 4), ("y", -3), ("s", 2), ("r2", 0), ("r1", 2),
+    ("s", 3), ("r2", 1), ("r3", 0), ("r1", 3), ("r2", 2), ("r3", 1), ("r4", 0),
+    ("r2", 3), ("r3", 2), ("r4", 1), ("r3", 3), ("r4", 2), ("ta", 0), ("act", 1),
+    ("r4", 3), ("act", 2), ("ta", 1), ("c1", 1), ("act", 0), ("c1", 2), ("c2", 1),
+    ("ta", 2), ("act", 3), ("c2", 2), ("c3", 1), ("ta", 3), ("c1", 3), ("c3", 2),
+    ("c1", 0), ("c2", 3), ("p", 1), ("c2", 0), ("p", 2), ("c3", 3), ("m", 1),
+    ("c3", 0), ("m", 2), ("p", 3), ("z", 1), ("p", 0), ("z", 2), ("m", 3),
+    ("m", 0), ("z", 3), ("z", 0), ("g", 0), ("g", 1), ("g", 2), ("g", 3),
 )
 
 
@@ -121,10 +120,11 @@
         for copy in flow[offset]:
             copy.wait_recv()
 
-    def share(slot):
-        across[slot].wait_recv()
-        mine = tok.at[:, slot, k]
-        shared[slot] = send("share", mine, mine, sibling)
+    def share(c):
+        for slot in (2 * c, 2 * c + 1):
+            across[slot].wait_recv()
+        mine = tok.at[:, 2 * c : 2 * c + 2, k]
+        shared[c] = send("share", mine, mine, sibling)
 
     wave = {}
 
@@ -132,8 +132,7 @@
         act_t[:, c * 8 * BLK : (c + 1) * 8 * BLK] = rows_of(tok[0, 2 * c : 2 * c + 2]).T
 
     def reduce1(c):
-        for slot in (2 * c, 2 * c + 1):
-            shared[slot].wait_recv()
+        shared[c].wait_recv()
         for a in range(2):
             i, f = 2 * c + a, (f1x, f2x)[a]
             rows = rows_of(tok[a, 2 * c : 2 * c + 2])

time: 86.6 us -> 86.8 us (level)
  no operation moved by 1% of the time
where the time goes in v8:
time: 86.8 us; the launch traced here: 86.3 us
  Pallas kernels  85.6 us (99%)
    pallas_call x1, Pallas kernels, shards(): pl.pallas_call(kernel, out_shape=(small, small, large, large), in_specs=[...  83.1 us
    pallas_call x1, Pallas kernels, shards(): pl.pallas_call(place, out_shape=(large, large, small, small), in_specs=[p...  2.53 us

profile of v8, /device:TPU:6, one launch (start us, length us, event | category | flops | bytes accessed | tf_op | source)
XLA Modules:
  0.0 86.3 jit_solution(3469199671893681069)
XLA Ops:
  0.6 83.1 %layer.1 = (bf16[16,768]{1,0:T(8,128)(2,1)}, bf16[16,768]{1,0:T(8,128)(2,1)}, bf16[768,768]{1,0:T(8,128)(2,1)}, bf16[768,768]{1,0:T(8,128)(2,1)}) custom-call(bf16[16,768]{1,0:T(8,128)(2,1)} %act_hbm.1, bf16[768,768]{1,0:T(8,128)(2,1)} %up_hbm.1, bf16[768,768]{1,0:T(8,128)(2,1)} %down_hbm.1, bf16[16,768]{1,0:T(8,128)(2,1)} %cot_hbm.1), custom_call_target="tpu_custom_call" | custom-call | flops 3623878656 | bytes 4718592 | tf_op jit(solution)/shard_map/layer/pallas_call | solution.py:360
  83.8 2.5 %place.1 = (bf16[768,768]{1,0:T(8,128)(2,1)}, bf16[768,768]{1,0:T(8,128)(2,1)}, bf16[16,768]{1,0:T(8,128)(2,1)}, bf16[16,768]{1,0:T(8,128)(2,1)}) custom-call(bf16[768,768]{1,0:T(8,128)(2,1)} %get-tuple-element.12.refs_0_, bf16[768,768]{1,0:T(8,128)(2,1)} %get-tuple-element.13.refs_1_, bf16[16,768]{1,0:T(8,128)(2,1)} %get-tuple-element.14.refs_2_, ...), custom_call_target="tpu_custom_call" | custom-call | tf_op jit(solution)/shard_map/place/pallas_call | solution.py:375
